TPU v7x, 32 devices: a whole 2x2x4 slice. The times are simulated.
32 devices in a mesh: tile: 8 (over y, x, core), sub: 4 (over z).
Axes of the slice: x: 2, y: 2, z: 4, core: 2. Of those that a mesh axis runs over, the one named last changes fastest.
Arguments:
- source: bfloat16 [131072, 128], P(('tile', 'sub')), may hold values from -6 to 6
- fetch_blocks: int32 [2, 32, 32], P(None, ('tile', 'sub')), may hold values from -1 to 63, as said below
- pixel_cells: int32 [4, 2560, 256], P(None, ('tile', 'sub')), may hold values from 0 to 4095, as said below
- pixel_weights: float32 [4, 2560, 256], P(None, ('tile', 'sub')), may hold values from 0.1 to 0.5
- seam_flip: int32 [8], replicated, may hold values from 0 to 1, as said below
- encode_weight: bfloat16 [128, 64], replicated, may hold values from -0.5 to 0.5
- encode_bias: float32 [64], replicated, may hold values from -3 to 3
- first_kernel: bfloat16 [3, 3, 64, 64], replicated, may hold values from -0.25 to 0.25
- first_bias: float32 [64], replicated, may hold values from -3 to 3
- second_kernel: bfloat16 [3, 3, 64, 64], replicated, may hold values from -0.25 to 0.25
- second_bias: float32 [64], replicated, may hold values from -3 to 3
Outputs:
- features: bfloat16 [64, 2560, 256], P(None, ('tile', 'sub'))
Inputs may be any that keep to these rules, and one draw needn't show every extreme that they name: fetch_blocks[c, d, q] is the block among device q's 64 source blocks that device d requests in slot c, or -1 for an empty slot; the live slots of a pair come first and name distinct blocks; every device has some live slot, and in every draw some device fills all 2 slots from every device. `pixel_cells`: an entry f of a pixel on device d names cell f % 64 of the block that d requests in slot f // (32 * 64) from device (f // 64) % 32, and that slot is never empty. `seam_flip`: both values occur in every draw.
All inputs are finite; a program needn't handle non-finite values.
Results may differ from a plain program's by a relative error of at most 0.0053.
Values may be sent and summed in bfloat16 or wider, within the bound.
A program may use at most 128 MiB of HBM per device.

v0:
```python
import jax
import jax.numpy as jnp
from jax import lax
from jax.sharding import PartitionSpec as P

V = 128
CH = 64
SB = 64
SBLK = 64


def with_halo(block, sides, width, periodic):
    for axis, dim in sides:
        count = lax.axis_size(axis)
        forward = [(i, i + 1) for i in range(count - 1)]
        if periodic:
            forward.append((count - 1, 0))
        backward = [(target, source) for source, target in forward]
        low = lax.ppermute(
            lax.slice_in_dim(block, block.shape[dim] - width, None, axis=dim), axis, forward
        )
        high = lax.ppermute(lax.slice_in_dim(block, 0, width, axis=dim), axis, backward)
        block = jnp.concatenate([low, block, high], axis=dim)
    return block


def swapped(value, axis, bit):
    return lax.ppermute(value, axis, [(i, i ^ 1 << bit) for i in range(lax.axis_size(axis))])


def select_blocks(stored, wanted):
    present = wanted >= 0
    chosen = jnp.take(stored, jnp.maximum(wanted, 0), axis=0)
    return jnp.where(present[..., None, None], chosen, jnp.zeros((), stored.dtype))


def fetch_fields(source, fetch_blocks):
    stored = source.reshape(SBLK, SB, V)
    arrived = lax.all_to_all(
        select_blocks(
            stored,
            lax.all_to_all(fetch_blocks, ("tile", "sub"), split_axis=2, concat_axis=1, tiled=True),
        ),
        ("tile", "sub"),
        split_axis=1,
        concat_axis=2,
        tiled=True,
    )
    return arrived.reshape(-1, V)


def encode_pixels(pooled, pixel_cells, pixel_weights, encode_weight, encode_bias):
    term_count, row_count, col_count = pixel_cells.shape
    stride = 16

    def encode_one_block(block_index, encoded):
        first_row = block_index * stride
        cell_ids = lax.dynamic_slice_in_dim(pixel_cells, first_row, stride, 1).reshape(-1)
        weights = lax.dynamic_slice_in_dim(pixel_weights, first_row, stride, 1).reshape(
            term_count, -1, 1
        )
        fetched = jnp.take(pooled, cell_ids, axis=0).reshape(term_count, -1, V)
        regridded = jnp.sum(weights * fetched.astype(jnp.float32), axis=0).astype(jnp.bfloat16)
        projected = lax.dot_general(
            encode_weight, regridded, (((0,), (1,)), ((), ())), preferred_element_type=jnp.float32
        )
        piece_out = (
            (projected + encode_bias[:, None]).astype(jnp.bfloat16).reshape(CH, stride, col_count)
        )
        return lax.dynamic_update_slice_in_dim(encoded, piece_out, first_row, 1)

    return lax.fori_loop(
        0,
        row_count // stride,
        encode_one_block,
        jnp.zeros((CH, row_count, col_count), jnp.bfloat16),
    )


def seam_turns(seam_flip):
    tile_count = lax.axis_size("tile")
    tile_index = lax.axis_index("tile")
    positions = jnp.arange(tile_count, dtype=jnp.int32)
    right_flip = jnp.sum(jnp.where(positions == tile_index, seam_flip, 0)) > 0
    left_flip = (
        jnp.sum(jnp.where(positions == (tile_index + tile_count - 1) % tile_count, seam_flip, 0))
        > 0
    )
    return (left_flip, right_flip)


def pad_tiles(feature_map, margin, seam_state):
    extended = with_halo(feature_map, (("sub", 1),), margin, False)
    borders = jnp.stack((extended[:, :, :margin], extended[:, :, -margin:]))
    borders = jnp.transpose(borders, (0, 3, 1, 2))
    turned = borders[..., ::-1]
    for bit_number in range(lax.axis_size("sub").bit_length() - 1):
        turned = swapped(turned, "sub", bit_number)
    outgoing = jnp.concatenate(
        (
            jnp.where(seam_state[0], turned[0], borders[0]),
            jnp.where(seam_state[1], turned[1], borders[1]),
        ),
        axis=0,
    )
    beside_all = with_halo(outgoing, (("tile", 0),), margin, True)
    leading = jnp.transpose(beside_all[:margin], (1, 2, 0))
    trailing = jnp.transpose(beside_all[-margin:], (1, 2, 0))
    return jnp.concatenate((leading, extended, trailing), axis=2)


def kernel_matrix(kernel):
    return jnp.transpose(kernel, (2, 0, 1, 3)).reshape(kernel.shape[2], -1)


def conv_window(padded, matrix, first_row, height, col_count):
    window = lax.dynamic_slice_in_dim(padded, first_row, height + 2, 1)
    shifted = [
        window[:, row_tap : row_tap + height, col_tap : col_tap + col_count]
        for row_tap in range(3)
        for col_tap in range(3)
    ]
    stacked = jnp.concatenate(shifted, axis=0).reshape(-1, height * col_count)
    return jnp.dot(matrix, stacked, preferred_element_type=jnp.float32).reshape(
        -1, height, col_count
    )


def conv_rows(padded, matrix, row_count, col_count, finish):
    stride = min(8, row_count)

    def conv_one_block(block_index, result):
        first_row = block_index * stride
        piece_out = finish(
            conv_window(padded, matrix, first_row, stride, col_count), first_row, stride
        )
        return lax.dynamic_update_slice_in_dim(result, piece_out, first_row, 1)

    return lax.fori_loop(
        0,
        row_count // stride,
        conv_one_block,
        jnp.zeros((matrix.shape[0], row_count, col_count), jnp.bfloat16),
    )


def shards(
    source,
    fetch_blocks,
    pixel_cells,
    pixel_weights,
    seam_flip,
    encode_weight,
    encode_bias,
    first_kernel,
    first_bias,
    second_kernel,
    second_bias,
):
    pooled = fetch_fields(source, fetch_blocks)
    encoded = encode_pixels(pooled, pixel_cells, pixel_weights, encode_weight, encode_bias)
    row_count, col_count = (encoded.shape[1], encoded.shape[2])
    seam_state = seam_turns(seam_flip)
    first_matrix = kernel_matrix(first_kernel)
    second_matrix = kernel_matrix(second_kernel)

    def activate(summed, first_row, height):
        return jax.nn.silu(summed + first_bias[:, None, None]).astype(jnp.bfloat16)

    def finish_output(summed, first_row, height):
        residual = lax.dynamic_slice_in_dim(encoded, first_row, height, 1).astype(jnp.float32)
        return (summed + second_bias[:, None, None] + residual).astype(jnp.bfloat16)

    hidden = conv_rows(
        pad_tiles(encoded, 1, seam_state), first_matrix, row_count, col_count, activate
    )
    hidden_padded = pad_tiles(hidden, 1, seam_state)
    return conv_rows(hidden_padded, second_matrix, row_count, col_count, finish_output)


def solution(mesh):
    in_specs = (
        P(("tile", "sub"), None),
        P(None, ("tile", "sub"), None),
        P(None, ("tile", "sub"), None),
        P(None, ("tile", "sub"), None),
        P(),
        P(),
        P(),
        P(),
        P(),
        P(),
        P(),
    )
    out_specs = P(None, ("tile", "sub"), None)
    return jax.shard_map(shards, mesh=mesh, in_specs=in_specs, out_specs=out_specs, check_vma=False)
```

profile of v0, /device:TPU:0, one launch (start us, length us, event | category | flops | bytes accessed | tf_op | source)
XLA Modules:
  0.0 802.9 jit_solution(1503677598681900644)
XLA Ops:
  0.9 14.3 %all_to_all.8 = s32[2,1,32]{0,1,2:T(1,128)S(1)} all-to-all(s32[2,1,32]{0,1,2:T(1,128)S(1)} %copy.101), channel_id=1, replica_groups=mesh['tile'=8,'sub'=4] {'tile','sub'}, dimensions={2} | all-to-all | bytes 512 | tf_op jit(solution)/shard_map/all_to_all | solution.py:42
  17.4 2.6 all-to-all-start.1
  20.0 25.0 %all-to-all-done.1 = bf16[2,32,1,64,128]{4,3,0,2,1:T(8,128)(2,1)S(1)} async-done(((bf16[2,32,1,64,128]{4,3,0,2,1:T(8,128)(2,1)}), bf16[2,32,1,64,128]{4,3,0,2,1:T(8,128)(2,1)S(1)}, u32[]{:S(2)}, u32[]{:S(2)}) %all-to-all-start.1) | async-done | bytes 1048608 | tf_op jit(solution)/shard_map/all_to_all | solution.py:39
  46.8 343.5 %while.39 = (s32[]{:T(128)}, bf16[64,80,256]{2,1,0:T(8,128)(2,1)}, f32[4,80,256]{2,1,0:T(8,128)}, s32[4,80,256]{2,1,0:T(8,128)}, bf16[4096,128]{1,0:T(8,128)(2,1...) while((s32[]{:T(128)}, bf16[64,80,256]{2,1,0:T(8,128)(2,1)}, ...), condition=%wide.region_3.4_spmd, body=%wide.region_1.3_spmd.sunk | while | flops 75661320 | bytes 18596268 | solution.py:72
  47.8 57.4 %gather_fusion = bf16[16384,128]{1,0:T(8,128)(2,1)} fusion(bf16[4096,128]{1,0:T(8,128)(2,1)S(1)} %get-tuple-element.584, s32[16384]{0:T(1024)S(1)} %broadcast_clamp_fusion.2), kind=kCustom, calls=%fused_computation.clone.1 | custom fusion | bytes 8454144 | tf_op jit(solution)/shard_map/while/body/eval_jaxpr/jit(_take)/gather | solution.py:62
  107.1 6.9 multiply_reduce_fusion.2
  116.5 57.4 %gather_fusion = bf16[16384,128]{1,0:T(8,128)(2,1)} fusion(bf16[4096,128]{1,0:T(8,128)(2,1)S(1)} %get-tuple-element.584, s32[16384]{0:T(1024)S(1)} %broadcast_clamp_fusion.2), kind=kCustom, calls=%fused_computation.clone.1 | custom fusion | bytes 8454144 | tf_op jit(solution)/shard_map/while/body/eval_jaxpr/jit(_take)/gather | solution.py:62
  175.7 6.9 multiply_reduce_fusion.2
  185.2 57.4 %gather_fusion = bf16[16384,128]{1,0:T(8,128)(2,1)} fusion(bf16[4096,128]{1,0:T(8,128)(2,1)S(1)} %get-tuple-element.584, s32[16384]{0:T(1024)S(1)} %broadcast_clamp_fusion.2), kind=kCustom, calls=%fused_computation.clone.1 | custom fusion | bytes 8454144 | tf_op jit(solution)/shard_map/while/body/eval_jaxpr/jit(_take)/gather | solution.py:62
  244.5 6.9 multiply_reduce_fusion.2
  253.9 57.4 %gather_fusion = bf16[16384,128]{1,0:T(8,128)(2,1)} fusion(bf16[4096,128]{1,0:T(8,128)(2,1)S(1)} %get-tuple-element.584, s32[16384]{0:T(1024)S(1)} %broadcast_clamp_fusion.2), kind=kCustom, calls=%fused_computation.clone.1 | custom fusion | bytes 8454144 | tf_op jit(solution)/shard_map/while/body/eval_jaxpr/jit(_take)/gather | solution.py:62
  313.2 6.9 multiply_reduce_fusion.2
  322.6 57.4 %gather_fusion = bf16[16384,128]{1,0:T(8,128)(2,1)} fusion(bf16[4096,128]{1,0:T(8,128)(2,1)S(1)} %get-tuple-element.584, s32[16384]{0:T(1024)S(1)} %broadcast_clamp_fusion.2), kind=kCustom, calls=%fused_computation.clone.1 | custom fusion | bytes 8454144 | tf_op jit(solution)/shard_map/while/body/eval_jaxpr/jit(_take)/gather | solution.py:62
  381.9 6.9 multiply_reduce_fusion.2
  390.3 2.6 copy.106
  392.9 5.0 collective-permute-start
  399.3 6.3 copy.109
  405.5 6.8 copy.108
  412.4 6.8 copy.110
  420.2 2.7 collective-permute-start.2
  433.9 8.2 %pad_maximum_fusion = bf16[64,82,258]{1,0,2:T(8,128)(2,1)} fusion(bf16[64,82,1]{1,0,2:T(8,128)(2,1)S(1)} %bitcast.149, bf16[64,1,256]{1,0,2:T(8,128)(2,1)} %copy.110, bf16[64,80,256]{1,0,2:T(8,128)(2,1)} %copy.109, bf16[64,1,256]{1,0,2:T(8,128)(2,1)} %copy.108, bf16[64,82,1]{1,0,2:T(8,128)(2,1)S(1)} %bitcast.147), kind=kLoop, calls=%fused_computation.38 | loop fusion | flops 13539840 | bytes 5415936 | tf_op jit(solution)/shard_map/concatenate | solution.py:109
  442.1 7.9 copy.112
  451.7 140.6 %while.40 = (s32[]{:T(128)}, bf16[64,80,256]{2,1,0:T(8,128)(2,1)}, bf16[64,82,258]{2,1,0:T(8,128)(2,1)}, bf16[64,576]{1,0:T(8,128)(2,1)S(1)}, f32[64]{0:T(128)S(...) while((s32[]{:T(128)}, bf16[64,80,256]{2,1,0:T(8,128)(2,1)}, ...), condition=%wide.region_6.7_spmd, body=%wide.region_5.6_spmd.sunk | while | flops 151781392 | bytes 14230060 | solution.py:139
  594.9 3.9 collective-permute-start.6
  600.1 6.3 copy.117
  606.4 6.8 copy.116
  613.2 6.8 copy.118
  621.0 2.7 collective-permute-start.8
  627.1 3.3 collective-permute-done.9
  634.6 8.2 %pad_maximum_fusion.1 = bf16[64,82,258]{1,0,2:T(8,128)(2,1)} fusion(bf16[64,82,1]{1,0,2:T(8,128)(2,1)S(1)} %bitcast.150, bf16[64,1,256]{1,0,2:T(8,128)(2,1)} %copy.118, bf16[64,80,256]{1,0,2:T(8,128)(2,1)} %copy.117, bf16[64,1,256]{1,0,2:T(8,128)(2,1)} %copy.116, bf16[64,82,1]{1,0,2:T(8,128)(2,1)S(1)} %bitcast.148), kind=kLoop, calls=%fused_computation.39 | loop fusion | flops 13539840 | bytes 5415936 | tf_op jit(solution)/shard_map/concatenate | solution.py:109
  642.8 7.9 copy.120
  652.4 149.3 %while.41 = (s32[]{:T(128)}, bf16[64,80,256]{2,1,0:T(8,128)(2,1)}, bf16[64,82,258]{2,1,0:T(8,128)(2,1)}, bf16[64,576]{1,0:T(8,128)(2,1)S(1)}, f32[64]{0:T(128)S(...) while((s32[]{:T(128)}, bf16[64,80,256]{2,1,0:T(8,128)(2,1)}, ...), condition=%wide.region_8.9_spmd, body=%wide.region_7.8_spmd.sunk | while | flops 151519248 | bytes 14492212 | solution.py:139
  (386 shorter events, 343.6 us)
Async XLA Ops:
  0.0 15.3 %copy-start = (bf16[4096,128]{1,0:T(8,128)(2,1)S(1)}, bf16[4096,128]{1,0:T(8,128)(2,1)}, u32[]{:S(2)}) copy-start(bf16[4096,128]{1,0:T(8,128)(2,1)} %param.17) | copy-start | bytes 3145732
  17.4 27.7 %all-to-all-start.1 = ((bf16[2,32,1,64,128]{4,3,0,2,1:T(8,128)(2,1)}), bf16[2,32,1,64,128]{4,3,0,2,1:T(8,128)(2,1)S(1)}, u32[]{:S(2)}, u32[]{:S(2)}) async-start(bf16[2,32,1,64,128]{4,3,0,2,1:T(8,128)(2,1)} %copy.104), calls=%async_computation.1 | async-start | bytes 2097152 | tf_op jit(solution)/shard_map/all_to_all | solution.py:39
  20.0 26.8 %copy-start.2 = (bf16[128,64]{0,1:T(8,128)(2,1)S(1)}, bf16[128,64]{0,1:T(8,128)(2,1)}, u32[]{:S(2)}) copy-start(bf16[128,64]{0,1:T(8,128)(2,1)} %param.22) | copy-start | bytes 49156
  20.0 26.8 %copy-start.6 = (f32[64]{0:T(128)S(1)}, f32[64]{0:T(128)}, u32[]{:S(2)}) copy-start(f32[64]{0:T(128)} %param.23) | copy-start | bytes 772
  392.9 12.6 %collective-permute-start = (bf16[64,1,256]{2,0,1:T(8,128)(2,1)S(1)}, bf16[64,1,256]{2,0,1:T(8,128)(2,1)S(1)}, u32[]{:S(2)}, u32[]{:S(2)}) collective-permute-start(bf16[64,1,256]{2,0,1:T(8,128)(2,1)S(1)} %get-tuple-element.439), channel_id=1, source_target_pairs={{0,1},{1,2},{2,3},{4,5},{5,6},{6,7},{8,9},{9,10},{10,11},{12,13},{... | collective-permute-start | bytes 98312 | tf_op jit(solution)/shard_map/ppermute | solution.py:19
  398.0 14.4 %collective-permute-start.1 = (bf16[64,1,256]{2,0,1:T(8,128)(2,1)S(1)}, bf16[64,1,256]{2,0,1:T(8,128)(2,1)S(1)}, u32[]{:S(2)}, u32[]{:S(2)}) collective-permute-start(bf16[64,1,256]{2,0,1:T(8,128)(2,1)S(1)} %get-tuple-element.440), channel_id=1, source_target_pairs={{1,0},{2,1},{3,2},{5,4},{6,5},{7,6},{9,8},{10,9},{11,10},{13,12},{... | collective-permute-start | bytes 98312 | tf_op jit(solution)/shard_map/ppermute | solution.py:22
  419.1 7.1 copy-start.8
  419.1 13.2 %copy-start.3 = (bf16[3,3,64,64]{3,2,1,0:T(8,128)(2,1)S(1)}, bf16[3,3,64,64]{3,2,1,0:T(8,128)(2,1)}, u32[]{:S(2)}) copy-start(bf16[3,3,64,64]{3,2,1,0:T(8,128)(2,1)} %param.24) | copy-start | bytes 221188
  420.2 4.6 collective-permute-start.2
  424.8 4.8 collective-permute-start.3
  429.6 4.2 collective-permute-start.4
  429.7 4.2 collective-permute-start.5
  450.0 1.7 copy-start.7
  594.9 11.5 %collective-permute-start.6 = (bf16[64,1,256]{2,0,1:T(8,128)(2,1)S(1)}, bf16[64,1,256]{2,0,1:T(8,128)(2,1)S(1)}, u32[]{:S(2)}, u32[]{:S(2)}) collective-permute-start(bf16[64,1,256]{2,0,1:T(8,128)(2,1)S(1)} %get-tuple-element.437), channel_id=1, source_target_pairs={{0,1},{1,2},{2,3},{4,5},{5,6},{6,7},{8,9},{9,10},{10,11},{12,13},{... | collective-permute-start | bytes 98312 | tf_op jit(solution)/shard_map/ppermute | solution.py:19
  598.8 14.4 %collective-permute-start.7 = (bf16[64,1,256]{2,0,1:T(8,128)(2,1)S(1)}, bf16[64,1,256]{2,0,1:T(8,128)(2,1)S(1)}, u32[]{:S(2)}, u32[]{:S(2)}) collective-permute-start(bf16[64,1,256]{2,0,1:T(8,128)(2,1)S(1)} %get-tuple-element.438), channel_id=1, source_target_pairs={{1,0},{2,1},{3,2},{5,4},{6,5},{7,6},{9,8},{10,9},{11,10},{13,12},{... | collective-permute-start | bytes 98312 | tf_op jit(solution)/shard_map/ppermute | solution.py:22
  620.0 13.2 %copy-start.4 = (bf16[3,3,64,64]{3,2,1,0:T(8,128)(2,1)S(1)}, bf16[3,3,64,64]{3,2,1,0:T(8,128)(2,1)}, u32[]{:S(2)}) copy-start(bf16[3,3,64,64]{3,2,1,0:T(8,128)(2,1)} %param.26) | copy-start | bytes 221188
  621.0 4.6 collective-permute-start.8
  625.6 4.8 collective-permute-start.9
  630.5 4.1 collective-permute-start.10
  630.5 4.1 collective-permute-start.11
  650.7 1.7 copy-start.5
  801.7 1.2 copy-start.1
where the time goes:
time: 813 us; the launch traced here: 803 us
  local copies, waits for them, and re-layouts  626 us (77%)
  other arithmetic  81.7 us (10%)
  waiting for transfers between devices  36 us (4%)
  starting transfers between devices  27.9 us (3%)
  blocking collectives  14.3 us (2%)
  matrix products  13.9 us (2%)
    gather x5, local copies, waits for them, and re-layouts, encode_one_block(): fetched = jnp.take(pooled, cell_ids, axis=0).reshape(term_count, -1, V)  287 us
    while x225, local copies, waits for them, and re-layouts  232 us
    reduce_sum x5, other arithmetic, encode_one_block(): jnp.sum(weights * fetched.astype(jnp.float32), axis=0).astype(jnp.bfloat16)  34.6 us
    dynamic_update_slice x20, other arithmetic, conv_one_block(): return lax.dynamic_update_slice_in_dim(result, piece_out, first_row, 1)  27.2 us
    concatenate x20, local copies, waits for them, and re-layouts, conv_window(): stacked = jnp.concatenate(shifted, axis=0).reshape(-1, height * col_count)  27.1 us
    all_to_all x1, waiting for transfers between devices, fetch_fields(): lax.all_to_all(select_blocks(stored, lax.all_to_all(fetch_blocks, ('tile'...  25 us
    while x6, local copies, waits for them, and re-layouts, conv_rows(): lax.fori_loop(0, row_count // stride, conv_one_block, jnp.zeros((matrix.s...  25 us
    concatenate x2, other arithmetic, pad_tiles(): return jnp.concatenate((leading, extended, trailing), axis=2)  16.5 us
  transfers between devices with their start and end apart: 13, of which 7 were waited for; matrix products, arithmetic and copies ran while one was open for 3% of the time, Pallas kernels for 0%

commit v1 on v0

v1 whole, which is shorter than its diff:
```python
import functools

import jax
import jax.numpy as jnp
from jax import lax
from jax.experimental import pallas as pl
from jax.experimental.pallas import tpu as pltpu
from jax.sharding import PartitionSpec as P

SB = 64
LANES = 128
VMEM_LIMIT = 48 * 1024 * 1024


def vmem():
    return pl.BlockSpec(memory_space=pltpu.VMEM)


def smem():
    return pl.BlockSpec(memory_space=pltpu.SMEM)


def params():
    return pltpu.CompilerParams(vmem_limit_bytes=VMEM_LIMIT)


def project_kernel(wanted_ref, source_ref, weight_ref, out_ref, stored):
    tiles = source_ref.shape[0] // LANES
    half = weight_ref.shape[1] // 2
    low_lanes = lax.broadcasted_iota(jnp.int32, (half, LANES), 1) < SB

    def one_tile(t, carry):
        cells = source_ref[pl.ds(pl.multiple_of(t * LANES, LANES), LANES), :]
        x = lax.dot_general(
            weight_ref[...], cells, (((0,), (1,)), ((), ())), preferred_element_type=jnp.float32
        )
        top, bottom = x[:half], x[half:]
        stored[2 * t] = jnp.where(low_lanes, top, pltpu.roll(bottom, SB, 1)).astype(jnp.bfloat16)
        stored[2 * t + 1] = jnp.where(low_lanes, pltpu.roll(top, SB, 1), bottom).astype(
            jnp.bfloat16
        )
        return carry

    lax.fori_loop(0, tiles, one_tile, 0, unroll=4)

    def one_request(n, carry):
        w = wanted_ref[n]
        block = stored[jnp.maximum(w, 0)]
        out_ref[n] = jnp.where(w >= 0, block, jnp.zeros_like(block))
        return carry

    lax.fori_loop(0, out_ref.shape[0], one_request, 0, unroll=4)


def project_blocks(source, wanted, encode_weight):
    count = wanted.shape[0]
    blocks = source.shape[0] // SB
    half = encode_weight.shape[1] // 2
    return pl.pallas_call(
        project_kernel,
        out_shape=jax.ShapeDtypeStruct((count, half, LANES), jnp.bfloat16),
        in_specs=[smem(), vmem(), vmem()],
        out_specs=vmem(),
        scratch_shapes=[pltpu.VMEM((blocks, half, LANES), jnp.bfloat16)],
        compiler_params=params(),
    )(wanted, source, encode_weight)


def edge_insert(edge_ref, side, r, column):
    lane = lax.broadcasted_iota(jnp.int32, edge_ref.shape[1:], 1)
    edge_ref[side] = jnp.where(lane == r, column, edge_ref[side])


def spread(ref, k, r, first):
    base = pl.multiple_of(r // 8 * 8, 8)
    block = ref[k, pl.ds(base, 8), first : first + LANES]
    pick = jnp.full((8, LANES), r - base, jnp.int32)
    return jnp.take_along_axis(block, pick, axis=0, mode="promise_in_bounds")


def lookup_kernel(blocks_ref, cells_ref, weights_ref, bias_ref, out_ref, edge_ref, table, scales):
    terms, rows, cols = cells_ref.shape
    tiles, half = table.shape[0], table.shape[1]
    groups = half // 8
    low_lanes = lax.broadcasted_iota(jnp.int32, (half, LANES), 1) < SB

    def halves(t):
        first = blocks_ref[2 * t].astype(jnp.float32)
        second = blocks_ref[2 * t + 1].astype(jnp.float32)
        top = jnp.where(low_lanes, first, pltpu.roll(second, SB, 1))
        bottom = jnp.where(low_lanes, pltpu.roll(first, SB, 1), second)
        return top, bottom

    def largest(t, carry):
        top, bottom = halves(t)
        return jnp.maximum(carry[0], jnp.abs(top)), jnp.maximum(carry[1], jnp.abs(bottom))

    zero = jnp.zeros((half, LANES), jnp.float32)
    found = lax.fori_loop(0, tiles, largest, (zero, zero), unroll=4)
    tops = [jnp.maximum(jnp.max(m, axis=1, keepdims=True), 1e-30) for m in found]
    up = [jnp.broadcast_to(32000.0 / m, (half, LANES)) for m in tops]
    scales[0] = jnp.broadcast_to(tops[0] * (1.0 / 32000.0), (half, LANES))
    scales[1] = jnp.broadcast_to(tops[1] * (1.0 / 32000.0), (half, LANES))

    def pack(t, carry):
        top, bottom = halves(t)
        high = jnp.round(top * up[0]).astype(jnp.int32)
        low = jnp.round(bottom * up[1]).astype(jnp.int32)
        table[t] = (high << 16) | (low & 0xFFFF)
        return carry

    lax.fori_loop(0, tiles, pack, 0, unroll=2)
    edge_ref[...] = jnp.zeros_like(edge_ref)

    def one_row(r, carry):
        pieces = []
        for first in range(0, cols, LANES):
            index, tile, weight = [], [], []
            for k in range(terms):
                cell = spread(cells_ref, k, r, first)
                index.append(cell & (LANES - 1))
                tile.append(cell >> 7)
                weight.append(spread(weights_ref, k, r, first))
            got = [[jnp.zeros((8, LANES), jnp.int32)] * groups for _ in range(terms)]

            def some_tiles(t0, got):
                got = [list(g) for g in got]
                for dt in range(min(tiles, 32)):
                    t = t0 * min(tiles, 32) + dt
                    entries = [table[t, 8 * g : 8 * g + 8, :] for g in range(groups)]
                    for k in range(terms):
                        here = tile[k] == t
                        for g in range(groups):
                            value = jnp.take_along_axis(
                                entries[g], index[k], axis=1, mode="promise_in_bounds"
                            )
                            got[k][g] = jnp.where(here, value, got[k][g])
                return got

            if tiles <= 32:
                got = some_tiles(0, got)
            else:
                got = lax.fori_loop(0, tiles // 32, some_tiles, got)
            parts = [[], []]
            for g in range(groups):
                high = jnp.zeros((8, LANES), jnp.float32)
                low = jnp.zeros((8, LANES), jnp.float32)
                for k in range(terms):
                    high += (got[k][g] >> 16).astype(jnp.float32) * weight[k]
                    low += ((got[k][g] << 16) >> 16).astype(jnp.float32) * weight[k]
                parts[0].append(high * scales[0, 8 * g : 8 * g + 8, :])
                parts[1].append(low * scales[1, 8 * g : 8 * g + 8, :])
            pieces.append(jnp.concatenate(parts[0] + parts[1], axis=0) + bias_ref[...])
        value = jnp.concatenate(pieces, axis=1).astype(jnp.bfloat16)
        out_ref[r] = value
        edge_insert(edge_ref, 0, r, pieces[0][:, :1])
        edge_insert(edge_ref, 1, r, pieces[-1][:, LANES - 1 :])
        return carry

    lax.fori_loop(0, rows, one_row, 0)


def lookup(blocks, pixel_cells, pixel_weights, encode_bias):
    terms, rows, cols = pixel_cells.shape
    count, half, lanes = blocks.shape
    channels = 2 * half
    return pl.pallas_call(
        lookup_kernel,
        out_shape=(
            jax.ShapeDtypeStruct((rows, channels, cols), jnp.bfloat16),
            jax.ShapeDtypeStruct((2, channels, LANES), jnp.float32),
        ),
        in_specs=[vmem()] * 4,
        out_specs=(vmem(), vmem()),
        scratch_shapes=[
            pltpu.VMEM((count // 2, half, LANES), jnp.int32),
            pltpu.VMEM((2, half, LANES), jnp.float32),
        ],
        compiler_params=params(),
    )(blocks, pixel_cells, pixel_weights, encode_bias[:, None])


def conv_kernel(last, x_ref, top_ref, bottom_ref, side_ref, matrix_ref, bias_ref, *rest):
    if last:
        residual_ref, out_ref, stack = rest
    else:
        out_ref, edge_ref, stack = rest
        edge_ref[...] = jnp.zeros_like(edge_ref)
    rows, channels, cols = x_ref.shape
    lane = lax.broadcasted_iota(jnp.int32, (channels, cols), 1)
    side_lane = lax.broadcasted_iota(jnp.int32, (channels, LANES), 1)

    def build(p, row):
        wide = row.astype(jnp.float32)
        picked = [
            jnp.sum(jnp.where(side_lane == p, side_ref[s], 0.0), axis=1, keepdims=True)
            for s in range(2)
        ]
        left = jnp.where(lane == 0, picked[0], pltpu.roll(wide, 1, 1))
        right = jnp.where(lane == cols - 1, picked[1], pltpu.roll(wide, cols - 1, 1))
        stack[p, :channels] = left.astype(jnp.bfloat16)
        stack[p, channels : 2 * channels] = row
        stack[p, 2 * channels :] = right.astype(jnp.bfloat16)

    build(0, top_ref[...])
    build(rows + 1, bottom_ref[...])

    def fill(r, carry):
        build(r + 1, x_ref[r])
        return carry

    lax.fori_loop(0, rows, fill, 0, unroll=4)

    def one_row(r, carry):
        window = stack[pl.ds(r, 3)].reshape(9 * channels, cols)
        summed = (
            jnp.dot(matrix_ref[...], window, preferred_element_type=jnp.float32) + bias_ref[...]
        )
        if last:
            out_ref[r] = (summed + residual_ref[r].astype(jnp.float32)).astype(jnp.bfloat16)
        else:
            hidden = summed / (1.0 + jnp.exp(-summed))
            out_ref[r] = hidden.astype(jnp.bfloat16)
            edge_insert(edge_ref, 0, r, hidden[:, :1])
            edge_insert(edge_ref, 1, r, hidden[:, cols - 1 :])
        return carry

    lax.fori_loop(0, rows, one_row, 0, unroll=4)


def conv(x, halo, matrix, bias, residual=None):
    rows, channels, cols = x.shape
    last = residual is not None
    grid_shape = jax.ShapeDtypeStruct(x.shape, jnp.bfloat16)
    edge_shape = jax.ShapeDtypeStruct((2, channels, LANES), jnp.float32)
    operands = (x,) + halo + (matrix, bias[:, None]) + ((residual,) if last else ())
    return pl.pallas_call(
        functools.partial(conv_kernel, last),
        out_shape=grid_shape if last else (grid_shape, edge_shape),
        in_specs=[vmem()] * len(operands),
        out_specs=vmem() if last else (vmem(), vmem()),
        scratch_shapes=[pltpu.VMEM((rows + 2, 3 * channels, cols), jnp.bfloat16)],
        compiler_params=params(),
    )(*operands)


def halos(x, edges, seam_flip):
    rows = x.shape[0]
    subs, tiles = lax.axis_size("sub"), lax.axis_size("tile")
    sub, tile = lax.axis_index("sub"), lax.axis_index("tile")
    down = [(i, i + 1) for i in range(subs - 1)]
    up = [(i + 1, i) for i in range(subs - 1)]
    right = [(i, (i + 1) % tiles) for i in range(tiles)]
    left = [((i + 1) % tiles, i) for i in range(tiles)]
    top = lax.ppermute(x[rows - 1], "sub", down)
    bottom = lax.ppermute(x[0], "sub", up)
    edges = edges.astype(jnp.bfloat16)
    beside = jnp.stack(
        (lax.ppermute(edges[1], "tile", right), lax.ppermute(edges[0], "tile", left))
    )
    gathered = lax.all_gather(beside, "sub")[..., :rows]
    whole = jnp.moveaxis(gathered, 0, 2).reshape(2, x.shape[1], subs * rows)
    whole = jnp.pad(whole, ((0, 0), (0, 0), (1, 1)))
    flips = jnp.stack((seam_flip[(tile + tiles - 1) % tiles], seam_flip[tile]))
    whole = jnp.where(flips[:, None, None] > 0, whole[..., ::-1], whole)
    sides = lax.dynamic_slice_in_dim(whole, sub * rows, rows + 2, 2).astype(jnp.float32)
    sides = jnp.pad(sides, ((0, 0), (0, 0), (0, LANES - rows - 2)))
    return top, bottom, sides


def kernel_matrix(kernel):
    return jnp.transpose(kernel, (2, 0, 1, 3)).reshape(kernel.shape[2], -1)


def shards(
    source,
    fetch_blocks,
    pixel_cells,
    pixel_weights,
    seam_flip,
    encode_weight,
    encode_bias,
    first_kernel,
    first_bias,
    second_kernel,
    second_bias,
):
    wanted = lax.all_to_all(fetch_blocks, ("tile", "sub"), split_axis=2, concat_axis=1, tiled=True)
    slots, devices = wanted.shape[0], wanted.shape[1]
    chosen = project_blocks(source, wanted.reshape(-1), encode_weight)
    chosen = chosen.reshape((slots, devices) + chosen.shape[1:])
    arrived = lax.all_to_all(chosen, ("tile", "sub"), split_axis=1, concat_axis=1, tiled=True)
    blocks = arrived.reshape((-1,) + arrived.shape[2:])
    encoded, edges = lookup(blocks, pixel_cells, pixel_weights, encode_bias)
    hidden, hidden_edges = conv(
        encoded, halos(encoded, edges, seam_flip), kernel_matrix(first_kernel), first_bias
    )
    features = conv(
        hidden,
        halos(hidden, hidden_edges, seam_flip),
        kernel_matrix(second_kernel),
        second_bias,
        encoded,
    )
    return jnp.transpose(features, (1, 0, 2))


def solution(mesh):
    in_specs = (
        P(("tile", "sub"), None),
        P(None, ("tile", "sub"), None),
        P(None, ("tile", "sub"), None),
        P(None, ("tile", "sub"), None),
        P(),
        P(),
        P(),
        P(),
        P(),
        P(),
        P(),
    )
    out_specs = P(None, ("tile", "sub"), None)
    return jax.shard_map(shards, mesh=mesh, in_specs=in_specs, out_specs=out_specs, check_vma=False)
```

time: 813 us -> 290 us (0.36); the launches traced: 803 us -> 290 us
  local copies, waits for them, and re-layouts: 626 us -> 13.8 us
  Pallas kernels: 0 us -> 202 us
  other arithmetic: 81.7 us -> 1.65 us
  waiting for transfers between devices: 36 us -> 17.7 us
  matrix products: 13.9 us -> 0 us
  blocking collectives: 14.3 us -> 26.7 us
    gather x6 -> x0, local copies, waits for them, and re-layouts: 288 us -> none  [the longest x5 287 us: encode_one_block(): fetched = jnp.take(pooled, cell_ids, axis=0).reshape(term_count, -1, V)]
    while x233 -> x0, local copies, waits for them, and re-layouts: 266 us -> none
    pallas_call x0 -> x4, Pallas kernels: none -> 202 us  [the longest x1 169 us: lookup(): pl.pallas_call(lookup_kernel, out_shape=(jax.ShapeDtypeStruct((rows, chan...]
    reduce_sum x6 -> x0, other arithmetic: 35.3 us -> none  [the longest x5 34.6 us: encode_one_block(): jnp.sum(weights * fetched.astype(jnp.float32), axis=0).astype(jnp.bfloat16)]
    dynamic_update_slice x20 -> x0, other arithmetic: 27.2 us -> none  [conv_one_block(): return lax.dynamic_update_slice_in_dim(result, piece_out, first_row, 1)]
    ppermute x4 -> x0, local copies, waits for them, and re-layouts: 27.2 us -> none  [the longest x2 13.6 us: with_halo(): lax.ppermute(lax.slice_in_dim(block, block.shape[dim] - width, None, axis...]
    concatenate x20 -> x0, local copies, waits for them, and re-layouts: 27.1 us -> none  [conv_window(): stacked = jnp.concatenate(shifted, axis=0).reshape(-1, height * col_count)]
    all_gather x0 -> x2, blocking collectives: none -> 26.7 us  [halos(): gathered = lax.all_gather(beside, 'sub')[..., :rows]]
  transfers between devices with their start and end apart: 13 -> 10, of which waited for: 7 -> 2; matrix products, arithmetic and copies ran while one was open for 3% -> 2% of each run, Pallas kernels for 0% -> 0%
where the time goes in v1:
time: 290 us
  Pallas kernels  202 us (70%)
  starting transfers between devices  27.5 us (9%)
  blocking collectives  26.7 us (9%)
  waiting for transfers between devices  17.7 us (6%)
  local copies, waits for them, and re-layouts  13.8 us (5%)
    pallas_call x1, Pallas kernels, lookup(): pl.pallas_call(lookup_kernel, out_shape=(jax.ShapeDtypeStruct((rows, chan...  169 us
    pallas_call x2, Pallas kernels, conv(): pl.pallas_call(functools.partial(conv_kernel, last), out_shape=grid_shape...  29.7 us
    all_gather x2, blocking collectives, halos(): gathered = lax.all_gather(beside, 'sub')[..., :rows]  26.7 us
    all_to_all x1, waiting for transfers between devices, shards(): lax.all_to_all(chosen, ('tile', 'sub'), split_axis=1, concat_axis=1, tile...  11.4 us
    ppermute x2, starting transfers between devices, halos(): top = lax.ppermute(x[rows - 1], 'sub', down)  9.63 us
    unnamed x32, local copies, waits for them, and re-layouts  7.79 us
    all_to_all x1, starting transfers between devices, shards(): lax.all_to_all(fetch_blocks, ('tile', 'sub'), split_axis=2, concat_axis=1...  7.3 us
    all_to_all x1, waiting for transfers between devices, shards(): lax.all_to_all(fetch_blocks, ('tile', 'sub'), split_axis=2, concat_axis=1...  6.27 us
  transfers between devices with their start and end apart: 10, of which 2 were waited for; matrix products, arithmetic and copies ran while one was open for 2% of the time, Pallas kernels for 0%

profile of v1, /device:TPU:0, one launch (start us, length us, event | category | flops | bytes accessed | tf_op | source)
XLA Modules:
  0.0 289.8 jit_solution(232932308896517293)
XLA Ops:
  0.0 1.4 copy.47
  1.4 7.3 %all-to-all-start = ((s32[2,1,32]{0,1,2:T(1,128)}), s32[2,1,32]{0,1,2:T(1,128)S(1)}, u32[]{:S(2)}, u32[]{:S(2)}) async-start(s32[2,1,32]{0,1,2:T(1,128)} %copy.47), calls=%async_computation | async-start | bytes 32768 | tf_op jit(solution)/shard_map/all_to_all | solution.py:288
  8.7 0.8 copy.49.weight_ref
  9.6 6.3 %all-to-all-done = s32[2,1,32]{0,1,2:T(1,128)S(1)} async-done(((s32[2,1,32]{0,1,2:T(1,128)}), s32[2,1,32]{0,1,2:T(1,128)S(1)}, u32[]{:S(2)}, u32[]{:S(2)}) %all-to-all-start) | async-done | bytes 288 | tf_op jit(solution)/shard_map/all_to_all | solution.py:288
  16.0 1.2 copy-done.3
  17.2 3.2 %shard_map.109 = bf16[64,32,128]{2,1,0:T(8,128)(2,1)S(1)} custom-call(s32[64]{0:T(128)S(1)} %reshape.41.wanted_ref, bf16[4096,128]{1,0:T(8,128)(2,1)S(1)} %copy-done.3, bf16[128,64]{1,0:T(8,128)(2,1)S(1)} %copy.49.weight_ref), custom_call_target="tpu_custom_call" | custom-call | tf_op jit(solution)/shard_map/pallas_call | solution.py:59
  20.4 0.9 copy.50
  21.3 2.6 all-to-all-start.1
  24.2 0.1 copy.54
  24.3 0.1 copy.55.matrix_ref
  24.5 0.1 copy.58
  24.6 0.1 copy.59.matrix_ref
  24.8 0.7 fusion
  25.5 1.4 add_compare_fusion
  26.9 11.4 %all-to-all-done.1 = bf16[2,32,32,128]{3,2,0,1:T(8,128)(2,1)S(1)} async-done(((bf16[2,32,32,128]{3,2,0,1:T(8,128)(2,1)}), bf16[2,32,32,128]{3,2,0,1:T(8,128)(2,1)S(1)}, u32[]{:S(2)}, u32[]{:S(2)}) %all-to-all-start.1) | async-done | bytes 524320 | tf_op jit(solution)/shard_map/all_to_all | solution.py:292
  38.3 169.3 %shard_map.110 = (bf16[80,64,256]{2,1,0:T(8,128)(2,1)S(1)}, f32[2,64,128]{2,1,0:T(8,128)S(1)}) custom-call(bf16[64,32,128]{2,1,0:T(8,128)(2,1)S(1)} %bitcast.45, s32[4,80,256]{2,1,0:T(8,128)S(1)} %copy-done.4, f32[4,80,256]{2,1,0:T(8,128)S(1)} %copy-done.5, f32[64,1]{1,0:T(8,128)S(1)} %copy.52.bias_ref), custom_call_target="tpu_custom_call" | custom-call | tf_op jit(solution)/shard_map/pallas_call | solution.py:167
  207.6 1.2 collective-permute-start.2
  208.8 1.5 collective-permute-start.3
  210.3 1.3 collective-permute-start.1
  211.6 5.1 %collective-permute-start = (bf16[64,256]{1,0:T(8,128)(2,1)S(1)}, bf16[64,256]{1,0:T(8,128)(2,1)S(1)}, u32[]{:S(2)}, u32[]{:S(2)}) collective-permute-start(bf16[64,256]{1,0:T(8,128)(2,1)S(1)} %get-tuple-element.16), channel_id=1, source_target_pairs={{0,1},{1,2},{2,3},{4,5},{5,6},{6,7},{8,9},{9,10},{10,11},{12,13},{... | collective-permute-start | bytes 98312 | tf_op jit(solution)/shard_map/ppermute | solution.py:255
  216.7 13.3 %all-gather = bf16[8,64,128]{2,1,0:T(8,128)(2,1)S(1)} all-gather(bf16[2,64,128]{2,1,0:T(8,128)(2,1)S(1)} %pad_maximum_fusion), channel_id=2, replica_groups=mesh['tile'=8,'sub'=4] {'sub'}, dimensions={0}, use_global_device_ids=true | all-gather | bytes 163840 | tf_op jit(solution)/shard_map/all_gather | solution.py:261
  230.4 0.3 reverse
  231.0 15.0 %shard_map.111 = (bf16[80,64,256]{2,1,0:T(8,128)(2,1)S(1)}, f32[2,64,128]{2,1,0:T(8,128)S(1)}) custom-call(bf16[80,64,256]{2,1,0:T(8,128)(2,1)S(1)} %get-tuple-element.9.x_ref.rest_0_, bf16[64,256]{1,0:T(8,128)(2,1)S(1)} %collective-permute-done.top_ref, bf16[64,256]{1,0:T(8,128)(2,1)S(1)} %collective-permute-done.1.bottom_ref, ...), custom_call_target="tpu_custom_call" | custom-call | tf_op jit(solution)/shard_map/pallas_call | solution.py:237
  246.1 2.6 collective-permute-start.7
  248.8 1.5 copy-done.1
  250.3 1.3 collective-permute-start.5
  251.5 4.5 %collective-permute-start.4 = (bf16[64,256]{1,0:T(8,128)(2,1)S(1)}, bf16[64,256]{1,0:T(8,128)(2,1)S(1)}, u32[]{:S(2)}, u32[]{:S(2)}) collective-permute-start(bf16[64,256]{1,0:T(8,128)(2,1)S(1)} %get-tuple-element.14), channel_id=1, source_target_pairs={{0,1},{1,2},{2,3},{4,5},{5,6},{6,7},{8,9},{9,10},{10,11},{12,13},{... | collective-permute-start | bytes 98312 | tf_op jit(solution)/shard_map/ppermute | solution.py:255
  256.1 13.4 %all-gather.1 = bf16[8,64,128]{2,1,0:T(8,128)(2,1)S(1)} all-gather(bf16[2,64,128]{2,1,0:T(8,128)(2,1)S(1)} %pad_maximum_fusion.1), channel_id=3, replica_groups=mesh['tile'=8,'sub'=4] {'sub'}, dimensions={0}, use_global_device_ids=true | all-gather | bytes 163840 | tf_op jit(solution)/shard_map/all_gather | solution.py:261
  269.8 0.3 reverse.1
  270.5 1.7 copy-done.2
  272.2 14.6 %shard_map.112 = bf16[80,64,256]{2,1,0:T(8,128)(2,1)S(1)} custom-call(bf16[80,64,256]{2,1,0:T(8,128)(2,1)S(1)} %copy-done.2, bf16[64,256]{1,0:T(8,128)(2,1)S(1)} %collective-permute-done.4.top_ref, bf16[64,256]{1,0:T(8,128)(2,1)S(1)} %collective-permute-done.5.bottom_ref, f32[2,64,128]{2,1,0:T(8,128)S(1)} %pad_convert_fusion.side_ref, ...), custom_call_target="tpu_custom_call" | custom-call | tf_op jit(solution)/shard_map/pallas_call | solution.py:237
  286.8 3.0 %copy.61 = bf16[64,80,256]{2,1,0:T(8,128)(2,1)} copy(bf16[64,80,256]{2,0,1:T(8,128)(2,1)S(1)} %bitcast.44) | data formatting | bytes 5242880 | tf_op jit(solution)/shard_map/transpose | solution.py:305
  (56 shorter events, 1.7 us)
Async XLA Ops:
  0.0 23.9 %copy-start.9 = (f32[64]{0:T(128)S(1)}, f32[64]{0:T(128)}, u32[]{:S(2)}) copy-start(f32[64]{0:T(128)} %param.17) | copy-start | bytes 772
  0.0 24.0 %copy-start.10 = (f32[64]{0:T(128)S(1)}, f32[64]{0:T(128)}, u32[]{:S(2)}) copy-start(f32[64]{0:T(128)} %param.19) | copy-start | bytes 772
  0.0 24.1 %copy-start.11 = (f32[64]{0:T(128)S(1)}, f32[64]{0:T(128)}, u32[]{:S(2)}) copy-start(f32[64]{0:T(128)} %param.21) | copy-start | bytes 772
  0.0 24.8 %copy-start.8 = (s32[8]{0:T(128)S(1)}, s32[8]{0:T(128)}, u32[]{:S(2)}) copy-start(s32[8]{0:T(128)} %param.15) | copy-start | bytes 100
  1.4 14.4 %all-to-all-start = ((s32[2,1,32]{0,1,2:T(1,128)}), s32[2,1,32]{0,1,2:T(1,128)S(1)}, u32[]{:S(2)}, u32[]{:S(2)}) async-start(s32[2,1,32]{0,1,2:T(1,128)} %copy.47), calls=%async_computation | async-start | bytes 32768 | tf_op jit(solution)/shard_map/all_to_all | solution.py:288
  16.0 1.2 copy-start.3
  17.2 7.0 %copy-start.6 = (bf16[3,3,64,64]{3,2,1,0:T(8,128)(2,1)S(1)}, bf16[3,3,64,64]{3,2,1,0:T(8,128)(2,1)}, u32[]{:S(2)}) copy-start(bf16[3,3,64,64]{3,2,1,0:T(8,128)(2,1)} %param.18) | copy-start | bytes 221188
  17.2 7.3 %copy-start.7 = (bf16[3,3,64,64]{3,2,1,0:T(8,128)(2,1)S(1)}, bf16[3,3,64,64]{3,2,1,0:T(8,128)(2,1)}, u32[]{:S(2)}) copy-start(bf16[3,3,64,64]{3,2,1,0:T(8,128)(2,1)} %param.20) | copy-start | bytes 221188
  17.2 21.1 %copy-start.4 = (s32[4,80,256]{2,1,0:T(8,128)S(1)}, s32[4,80,256]{2,1,0:T(8,128)}, u32[]{:S(2)}) copy-start(s32[4,80,256]{2,1,0:T(8,128)} %cells_ref.1) | copy-start | bytes 983044
  17.2 21.1 %copy-start.5 = (f32[4,80,256]{2,1,0:T(8,128)S(1)}, f32[4,80,256]{2,1,0:T(8,128)}, u32[]{:S(2)}) copy-start(f32[4,80,256]{2,1,0:T(8,128)} %weights_ref.1) | copy-start | bytes 983044
  21.3 17.0 %all-to-all-start.1 = ((bf16[2,32,32,128]{3,2,0,1:T(8,128)(2,1)}), bf16[2,32,32,128]{3,2,0,1:T(8,128)(2,1)S(1)}, u32[]{:S(2)}, u32[]{:S(2)}) async-start(bf16[2,32,32,128]{3,2,0,1:T(8,128)(2,1)} %copy.50), calls=%async_computation.1 | async-start | bytes 1048576 | tf_op jit(solution)/shard_map/all_to_all | solution.py:292
  207.6 61.9 %copy-start = (bf16[80,64,256]{2,1,0:T(8,128)(2,1)}, bf16[80,64,256]{2,1,0:T(8,128)(2,1)S(1)}, u32[]{:S(2)}) copy-start(bf16[80,64,256]{2,1,0:T(8,128)(2,1)S(1)} %get-tuple-element.9.x_ref.rest_0_) | copy-start | bytes 7864324
  207.6 9.1 %collective-permute-start.2 = (bf16[64,128]{1,0:T(8,128)(2,1)S(1)}, bf16[64,128]{1,0:T(8,128)(2,1)S(1)}, u32[]{:S(2)}, u32[]{:S(2)}) collective-permute-start(bf16[64,128]{1,0:T(8,128)(2,1)S(1)} %get-tuple-element.19), channel_id=1, source_target_pairs={{0,4},{4,8},{8,12},{12,16},{16,20},{20,24},{24,28},{28,0},{1,5},{5... | collective-permute-start | bytes 49160 | tf_op jit(solution)/shard_map/ppermute | solution.py:259
  208.8 7.9 %collective-permute-start.3 = (bf16[64,128]{1,0:T(8,128)(2,1)S(1)}, bf16[64,128]{1,0:T(8,128)(2,1)S(1)}, u32[]{:S(2)}, u32[]{:S(2)}) collective-permute-start(bf16[64,128]{1,0:T(8,128)(2,1)S(1)} %get-tuple-element.20), channel_id=1, source_target_pairs={{4,0},{8,4},{12,8},{16,12},{20,16},{24,20},{28,24},{0,28},{5,1},{9... | collective-permute-start | bytes 49160 | tf_op jit(solution)/shard_map/ppermute | solution.py:259
  210.3 20.7 %collective-permute-start.1 = (bf16[64,256]{1,0:T(8,128)(2,1)S(1)}, bf16[64,256]{1,0:T(8,128)(2,1)S(1)}, u32[]{:S(2)}, u32[]{:S(2)}) collective-permute-start(bf16[64,256]{1,0:T(8,128)(2,1)S(1)} %get-tuple-element.15), channel_id=1, source_target_pairs={{1,0},{2,1},{3,2},{5,4},{6,5},{7,6},{9,8},{10,9},{11,10},{13,12},{... | collective-permute-start | bytes 98312 | tf_op jit(solution)/shard_map/ppermute | solution.py:256
  211.6 19.4 %collective-permute-start = (bf16[64,256]{1,0:T(8,128)(2,1)S(1)}, bf16[64,256]{1,0:T(8,128)(2,1)S(1)}, u32[]{:S(2)}, u32[]{:S(2)}) collective-permute-start(bf16[64,256]{1,0:T(8,128)(2,1)S(1)} %get-tuple-element.16), channel_id=1, source_target_pairs={{0,1},{1,2},{2,3},{4,5},{5,6},{6,7},{8,9},{9,10},{10,11},{12,13},{... | collective-permute-start | bytes 98312 | tf_op jit(solution)/shard_map/ppermute | solution.py:255
  246.1 10.0 %collective-permute-start.6 = (bf16[64,128]{1,0:T(8,128)(2,1)S(1)}, bf16[64,128]{1,0:T(8,128)(2,1)S(1)}, u32[]{:S(2)}, u32[]{:S(2)}) collective-permute-start(bf16[64,128]{1,0:T(8,128)(2,1)S(1)} %get-tuple-element.17), channel_id=1, source_target_pairs={{0,4},{4,8},{8,12},{12,16},{16,20},{20,24},{24,28},{28,0},{1,5},{5... | collective-permute-start | bytes 49160 | tf_op jit(solution)/shard_map/ppermute | solution.py:259
  246.1 10.0 %collective-permute-start.7 = (bf16[64,128]{1,0:T(8,128)(2,1)S(1)}, bf16[64,128]{1,0:T(8,128)(2,1)S(1)}, u32[]{:S(2)}, u32[]{:S(2)}) collective-permute-start(bf16[64,128]{1,0:T(8,128)(2,1)S(1)} %get-tuple-element.18), channel_id=1, source_target_pairs={{4,0},{8,4},{12,8},{16,12},{20,16},{24,20},{28,24},{0,28},{5,1},{9... | collective-permute-start | bytes 49160 | tf_op jit(solution)/shard_map/ppermute | solution.py:259
  248.8 1.5 copy-start.1
  250.3 20.2 %collective-permute-start.5 = (bf16[64,256]{1,0:T(8,128)(2,1)S(1)}, bf16[64,256]{1,0:T(8,128)(2,1)S(1)}, u32[]{:S(2)}, u32[]{:S(2)}) collective-permute-start(bf16[64,256]{1,0:T(8,128)(2,1)S(1)} %get-tuple-element.13), channel_id=1, source_target_pairs={{1,0},{2,1},{3,2},{5,4},{6,5},{7,6},{9,8},{10,9},{11,10},{13,12},{... | collective-permute-start | bytes 98312 | tf_op jit(solution)/shard_map/ppermute | solution.py:256
  251.5 18.9 %collective-permute-start.4 = (bf16[64,256]{1,0:T(8,128)(2,1)S(1)}, bf16[64,256]{1,0:T(8,128)(2,1)S(1)}, u32[]{:S(2)}, u32[]{:S(2)}) collective-permute-start(bf16[64,256]{1,0:T(8,128)(2,1)S(1)} %get-tuple-element.14), channel_id=1, source_target_pairs={{0,1},{1,2},{2,3},{4,5},{5,6},{6,7},{8,9},{9,10},{10,11},{12,13},{... | collective-permute-start | bytes 98312 | tf_op jit(solution)/shard_map/ppermute | solution.py:255
  270.4 1.7 copy-start.2

commit v2 on v1

v2 whole, which is shorter than its diff:
```python
import functools

import jax
import jax.numpy as jnp
from jax import lax
from jax.experimental import pallas as pl
from jax.experimental.pallas import tpu as pltpu
from jax.sharding import PartitionSpec as P

SB = 64
LANES = 128
VMEM_LIMIT = 48 * 1024 * 1024


def vmem():
    return pl.BlockSpec(memory_space=pltpu.VMEM)


def smem():
    return pl.BlockSpec(memory_space=pltpu.SMEM)


def params():
    return pltpu.CompilerParams(vmem_limit_bytes=VMEM_LIMIT)


def project_kernel(wanted_ref, source_ref, weight_ref, out_ref, stored):
    tiles = source_ref.shape[0] // LANES
    half = weight_ref.shape[1] // 2
    low_lanes = lax.broadcasted_iota(jnp.int32, (half, LANES), 1) < SB

    def one_tile(t, carry):
        cells = source_ref[pl.ds(pl.multiple_of(t * LANES, LANES), LANES), :]
        x = lax.dot_general(
            weight_ref[...], cells, (((0,), (1,)), ((), ())), preferred_element_type=jnp.float32
        )
        top, bottom = x[:half], x[half:]
        stored[2 * t] = jnp.where(low_lanes, top, pltpu.roll(bottom, SB, 1)).astype(jnp.bfloat16)
        stored[2 * t + 1] = jnp.where(low_lanes, pltpu.roll(top, SB, 1), bottom).astype(
            jnp.bfloat16
        )
        return carry

    lax.fori_loop(0, tiles, one_tile, 0, unroll=4)

    def one_request(n, carry):
        w = wanted_ref[n]
        block = stored[jnp.maximum(w, 0)]
        out_ref[n] = jnp.where(w >= 0, block, jnp.zeros_like(block))
        return carry

    lax.fori_loop(0, out_ref.shape[0], one_request, 0, unroll=4)


def project_blocks(source, wanted, encode_weight):
    count = wanted.shape[0]
    blocks = source.shape[0] // SB
    half = encode_weight.shape[1] // 2
    return pl.pallas_call(
        project_kernel,
        out_shape=jax.ShapeDtypeStruct((count, half, LANES), jnp.bfloat16),
        in_specs=[smem(), vmem(), vmem()],
        out_specs=vmem(),
        scratch_shapes=[pltpu.VMEM((blocks, half, LANES), jnp.bfloat16)],
        compiler_params=params(),
    )(wanted, source, encode_weight)


def edge_insert(edge_ref, side, r, column):
    lane = lax.broadcasted_iota(jnp.int32, edge_ref.shape[1:], 1)
    edge_ref[side] = jnp.where(lane == r + 1, column, edge_ref[side])


def spread(ref, k, r, first, height):
    base = pl.multiple_of(r // 8 * 8, 8)
    block = ref[k, pl.ds(base, 8), first : first + LANES]
    pick = jnp.full((8, LANES), r - base, jnp.int32)
    row = jnp.take_along_axis(block, pick, axis=0, mode="promise_in_bounds")
    return jnp.concatenate([row] * (height // 8), axis=0)


def lookup_kernel(blocks_ref, cells_ref, weights_ref, bias_ref, out_ref, edge_ref, table):
    terms, rows, cols = cells_ref.shape
    count, half = blocks_ref.shape[0], blocks_ref.shape[1]
    channels = 2 * half
    chunk, span = 4, 64
    low_lanes = lax.broadcasted_iota(jnp.int32, (half, LANES), 1) < SB

    def unpack(t, carry):
        first = blocks_ref[2 * t].astype(jnp.float32)
        second = blocks_ref[2 * t + 1].astype(jnp.float32)
        top = jnp.where(low_lanes, first, pltpu.roll(second, SB, 1))
        bottom = jnp.where(low_lanes, pltpu.roll(first, SB, 1), second)
        table[t] = jnp.concatenate((top, bottom), axis=0).astype(jnp.bfloat16)
        return carry

    lax.fori_loop(0, count // 2, unpack, 0, unroll=4)
    edge_ref[...] = jnp.zeros_like(edge_ref)
    within = lax.broadcasted_iota(jnp.int32, (SB, LANES), 0)
    zero = jnp.zeros((16, LANES), jnp.bfloat16)
    firsts = list(range(0, cols, LANES))

    def one_row(r, carry):
        block_of = [[None] * terms for _ in firsts]
        weighted = [[None] * terms for _ in firsts]
        for h, first in enumerate(firsts):
            for k in range(terms):
                inner = spread(cells_ref, k, r, first, SB) & (SB - 1)
                weight = spread(weights_ref, k, r, first, SB)
                block_of[h][k] = spread(cells_ref, k, r, first, 16) >> 6
                weighted[h][k] = jnp.where(inner == within, weight, 0.0).astype(jnp.bfloat16)

        def some_blocks(g, total):
            numbers = [
                [(b - g * span).astype(jnp.float32).astype(jnp.bfloat16) for b in side]
                for side in block_of
            ]
            for c in range(min(count, span) // chunk):
                halves = []
                for h in range(len(firsts)):
                    parts = []
                    for d in range(chunk):
                        number = jnp.asarray(c * chunk + d, jnp.bfloat16)
                        here = [numbers[h][k] == number for k in range(terms)]
                        for i in range(0, SB, 16):
                            found = [
                                jnp.where(here[k], weighted[h][k][i : i + 16], zero)
                                for k in range(terms)
                            ]
                            parts.append(sum(found[1:], found[0]))
                    halves.append(jnp.concatenate(parts, axis=0))
                at = (g * span + c * chunk) // 2
                lhs = jnp.concatenate([table[at + d] for d in range(chunk // 2)], axis=1)
                total = total + jnp.dot(
                    lhs, jnp.concatenate(halves, axis=1), preferred_element_type=jnp.float32
                )
            return total

        total = jnp.zeros((channels, cols), jnp.float32)
        if count <= span:
            total = some_blocks(0, total)
        else:
            total = lax.fori_loop(0, count // span, some_blocks, total)
        total = total + bias_ref[...]
        out_ref[r] = total.astype(jnp.bfloat16)
        edge_insert(edge_ref, 0, r, total[:, :1])
        edge_insert(edge_ref, 1, r, total[:, cols - 1 :])
        return carry

    lax.fori_loop(0, rows, one_row, 0)


def lookup(blocks, pixel_cells, pixel_weights, encode_bias):
    terms, rows, cols = pixel_cells.shape
    count, half, lanes = blocks.shape
    channels = 2 * half
    return pl.pallas_call(
        lookup_kernel,
        out_shape=(
            jax.ShapeDtypeStruct((rows, channels, cols), jnp.bfloat16),
            jax.ShapeDtypeStruct((2, channels, LANES), jnp.float32),
        ),
        in_specs=[vmem()] * 4,
        out_specs=(vmem(), vmem()),
        scratch_shapes=[pltpu.VMEM((count // 2, channels, LANES), jnp.bfloat16)],
        compiler_params=params(),
    )(blocks, pixel_cells, pixel_weights, encode_bias[:, None])


def conv_kernel(last, x_ref, top_ref, bottom_ref, side_ref, matrix_ref, bias_ref, *rest):
    if last:
        residual_ref, out_ref, taps = rest
    else:
        out_ref, edge_ref, taps = rest
        edge_ref[...] = jnp.zeros_like(edge_ref)
    rows, channels, cols = x_ref.shape
    lane = lax.broadcasted_iota(jnp.int32, (channels, cols), 1)
    side_lane = lax.broadcasted_iota(jnp.int32, (channels, LANES), 1)

    def multiply(p, row):
        wide = row.astype(jnp.float32)
        picked = [
            jnp.sum(jnp.where(side_lane == p, side_ref[s], 0.0), axis=1, keepdims=True)
            for s in range(2)
        ]
        left = jnp.where(lane == 0, picked[0], pltpu.roll(wide, 1, 1))
        right = jnp.where(lane == cols - 1, picked[1], pltpu.roll(wide, cols - 1, 1))
        beside = jnp.concatenate(
            (left.astype(jnp.bfloat16), row, right.astype(jnp.bfloat16)), axis=0
        )
        taps[p] = jnp.dot(matrix_ref[...], beside, preferred_element_type=jnp.float32)

    multiply(0, top_ref[...])
    multiply(rows + 1, bottom_ref[...])

    def fill(r, carry):
        multiply(r + 1, x_ref[r])
        return carry

    lax.fori_loop(0, rows, fill, 0, unroll=4)

    def one_row(r, carry):
        summed = bias_ref[...] + (
            taps[r, :channels]
            + taps[r + 1, channels : 2 * channels]
            + taps[r + 2, 2 * channels :]
        )
        if last:
            out_ref[r] = (summed + residual_ref[r].astype(jnp.float32)).astype(jnp.bfloat16)
        else:
            hidden = summed / (1.0 + jnp.exp(-summed))
            out_ref[r] = hidden.astype(jnp.bfloat16)
            edge_insert(edge_ref, 0, r, hidden[:, :1])
            edge_insert(edge_ref, 1, r, hidden[:, cols - 1 :])
        return carry

    lax.fori_loop(0, rows, one_row, 0, unroll=4)


def conv(x, halo, matrix, bias, residual=None):
    rows, channels, cols = x.shape
    last = residual is not None
    grid_shape = jax.ShapeDtypeStruct(x.shape, jnp.bfloat16)
    edge_shape = jax.ShapeDtypeStruct((2, channels, LANES), jnp.float32)
    operands = (x,) + halo + (matrix, bias[:, None]) + ((residual,) if last else ())
    return pl.pallas_call(
        functools.partial(conv_kernel, last),
        out_shape=grid_shape if last else (grid_shape, edge_shape),
        in_specs=[vmem()] * len(operands),
        out_specs=vmem() if last else (vmem(), vmem()),
        scratch_shapes=[pltpu.VMEM((rows + 2, 3 * channels, cols), jnp.float32)],
        compiler_params=params(),
    )(*operands)


def halos(x, edges, seam_flip):
    rows, channels, cols = x.shape
    subs, tiles = lax.axis_size("sub"), lax.axis_size("tile")
    tile = lax.axis_index("tile")
    down = [(i, i + 1) for i in range(subs - 1)]
    up = [(i + 1, i) for i in range(subs - 1)]
    top = lax.ppermute(x[rows - 1], "sub", down)
    bottom = lax.ppermute(x[0], "sub", up)
    lane = lax.broadcasted_iota(jnp.int32, (channels, LANES), 1)

    def side(s, step):
        c = (cols - 1) * s
        edge = edges[s].astype(jnp.bfloat16)
        edge = jnp.where(lane == 0, top[:, c : c + 1], edge)
        edge = jnp.where(lane == rows + 1, bottom[:, c : c + 1], edge)
        straight = [
            (t * subs + q, (t + step) % tiles * subs + q)
            for t in range(tiles)
            for q in range(subs)
        ]
        mirrored = [
            (t * subs + q, (t + step) % tiles * subs + subs - 1 - q)
            for t in range(tiles)
            for q in range(subs)
        ]
        return (
            lax.ppermute(edge, ("tile", "sub"), straight),
            lax.ppermute(edge, ("tile", "sub"), mirrored),
        )

    from_left, from_right = side(1, 1), side(0, -1)
    flips = (seam_flip[(tile + tiles - 1) % tiles], seam_flip[tile])
    chosen = []
    for (straight, mirrored), flip in zip((from_left, from_right), flips):
        turned = mirrored[:, : rows + 2][:, ::-1]
        turned = jnp.pad(turned, ((0, 0), (0, LANES - rows - 2)))
        chosen.append(jnp.where(flip > 0, turned, straight).astype(jnp.float32))
    return top, bottom, jnp.stack(chosen)


def kernel_matrix(kernel):
    size = kernel.shape[0] * kernel.shape[2]
    return jnp.transpose(kernel, (0, 2, 1, 3)).reshape(size, -1)


def shards(
    source,
    fetch_blocks,
    pixel_cells,
    pixel_weights,
    seam_flip,
    encode_weight,
    encode_bias,
    first_kernel,
    first_bias,
    second_kernel,
    second_bias,
):
    wanted = lax.all_to_all(fetch_blocks, ("tile", "sub"), split_axis=2, concat_axis=1, tiled=True)
    slots, devices = wanted.shape[0], wanted.shape[1]
    chosen = project_blocks(source, wanted.reshape(-1), encode_weight)
    chosen = chosen.reshape((slots, devices) + chosen.shape[1:])
    arrived = lax.all_to_all(chosen, ("tile", "sub"), split_axis=1, concat_axis=1, tiled=True)
    blocks = arrived.reshape((-1,) + arrived.shape[2:])
    encoded, edges = lookup(blocks, pixel_cells, pixel_weights, encode_bias)
    hidden, hidden_edges = conv(
        encoded, halos(encoded, edges, seam_flip), kernel_matrix(first_kernel), first_bias
    )
    features = conv(
        hidden,
        halos(hidden, hidden_edges, seam_flip),
        kernel_matrix(second_kernel),
        second_bias,
        encoded,
    )
    return jnp.transpose(features, (1, 0, 2))


def solution(mesh):
    in_specs = (
        P(("tile", "sub"), None),
        P(None, ("tile", "sub"), None),
        P(None, ("tile", "sub"), None),
        P(None, ("tile", "sub"), None),
        P(),
        P(),
        P(),
        P(),
        P(),
        P(),
        P(),
    )
    out_specs = P(None, ("tile", "sub"), None)
    return jax.shard_map(shards, mesh=mesh, in_specs=in_specs, out_specs=out_specs, check_vma=False)
```

time: 290 us -> 190 us (0.66)
  Pallas kernels: 202 us -> 110 us
  blocking collectives: 26.7 us -> 0 us
  waiting for transfers between devices: 17.7 us -> 29.9 us
  starting transfers between devices: 27.5 us -> 34.2 us
    pallas_call x1, Pallas kernels: 169 us -> 70.4 us  [lookup(): pl.pallas_call(lookup_kernel, out_shape=(jax.ShapeDtypeStruct((rows, chan...]
    all_gather x2 -> x0, blocking collectives: 26.7 us -> none  [halos(): gathered = lax.all_gather(beside, 'sub')[..., :rows]]
    pallas_call x2, Pallas kernels: 29.7 us -> 36.7 us  [conv(): pl.pallas_call(functools.partial(conv_kernel, last), out_shape=grid_shape...]
    ppermute x4 -> x8, waiting for transfers between devices: 0.01 us -> 6.61 us  [the longest x4 6.6 us: side(): lax.ppermute(edge, ('tile', 'sub'), mirrored)]
    ppermute x4 -> x8, starting transfers between devices: 5.39 us -> 11.9 us  [the longest x4 7.02 us: side(): lax.ppermute(edge, ('tile', 'sub'), straight)]
    unnamed x32 -> x26, local copies, waits for them, and re-layouts: 7.79 us -> 6.7 us
  transfers between devices with their start and end apart: 10 -> 14, of which waited for: 2 -> 7; matrix products, arithmetic and copies ran while one was open for 2% -> 2% of each run, Pallas kernels for 0% -> 0%
where the time goes in v2:
time: 190 us
  Pallas kernels  110 us (58%)
  starting transfers between devices  34.2 us (18%)
  waiting for transfers between devices  29.9 us (16%)
  local copies, waits for them, and re-layouts  13.3 us (7%)
    pallas_call x1, Pallas kernels, lookup(): pl.pallas_call(lookup_kernel, out_shape=(jax.ShapeDtypeStruct((rows, chan...  70.4 us
    pallas_call x2, Pallas kernels, conv(): pl.pallas_call(functools.partial(conv_kernel, last), out_shape=grid_shape...  36.7 us
    all_to_all x1, waiting for transfers between devices, shards(): lax.all_to_all(chosen, ('tile', 'sub'), split_axis=1, concat_axis=1, tile...  14.3 us
    ppermute x2, starting transfers between devices, halos(): top = lax.ppermute(x[rows - 1], 'sub', down)  9.65 us
    all_to_all x1, starting transfers between devices, shards(): lax.all_to_all(fetch_blocks, ('tile', 'sub'), split_axis=2, concat_axis=1...  7.3 us
    ppermute x4, starting transfers between devices, side(): lax.ppermute(edge, ('tile', 'sub'), straight)  7.02 us
    unnamed x26, local copies, waits for them, and re-layouts  6.7 us
    ppermute x4, waiting for transfers between devices, side(): lax.ppermute(edge, ('tile', 'sub'), mirrored)  6.6 us
  transfers between devices with their start and end apart: 14, of which 7 were waited for; matrix products, arithmetic and copies ran while one was open for 2% of the time, Pallas kernels for 0%

profile of v2, /device:TPU:0, one launch (start us, length us, event | category | flops | bytes accessed | tf_op | source)
XLA Modules:
  0.0 189.6 jit_solution(18094394418749029203)
XLA Ops:
  0.0 1.4 copy.37
  1.4 7.3 %all-to-all-start = ((s32[2,1,32]{0,1,2:T(1,128)}), s32[2,1,32]{0,1,2:T(1,128)S(1)}, u32[]{:S(2)}, u32[]{:S(2)}) async-start(s32[2,1,32]{0,1,2:T(1,128)} %copy.37), calls=%async_computation | async-start | bytes 32768 | tf_op jit(solution)/shard_map/all_to_all | solution.py:294
  8.7 0.8 copy.39.weight_ref
  9.5 6.3 %all-to-all-done = s32[2,1,32]{0,1,2:T(1,128)S(1)} async-done(((s32[2,1,32]{0,1,2:T(1,128)}), s32[2,1,32]{0,1,2:T(1,128)S(1)}, u32[]{:S(2)}, u32[]{:S(2)}) %all-to-all-start) | async-done | bytes 288 | tf_op jit(solution)/shard_map/all_to_all | solution.py:294
  15.9 1.2 copy-done.3
  17.2 3.2 %shard_map.109 = bf16[64,32,128]{2,1,0:T(8,128)(2,1)S(1)} custom-call(s32[64]{0:T(128)S(1)} %reshape.27.wanted_ref, bf16[4096,128]{1,0:T(8,128)(2,1)S(1)} %copy-done.3, bf16[128,64]{1,0:T(8,128)(2,1)S(1)} %copy.39.weight_ref), custom_call_target="tpu_custom_call" | custom-call | tf_op jit(solution)/shard_map/pallas_call | solution.py:59
  20.4 0.9 copy.40
  21.2 2.6 %all-to-all-start.1 = ((bf16[2,32,32,128]{3,2,0,1:T(8,128)(2,1)}), bf16[2,32,32,128]{3,2,0,1:T(8,128)(2,1)S(1)}, u32[]{:S(2)}, u32[]{:S(2)}) async-start(bf16[2,32,32,128]{3,2,0,1:T(8,128)(2,1)} %copy.40), calls=%async_computation.1 | async-start | bytes 1048576 | tf_op jit(solution)/shard_map/all_to_all | solution.py:298
  24.0 14.3 %all-to-all-done.1 = bf16[2,32,32,128]{3,2,0,1:T(8,128)(2,1)S(1)} async-done(((bf16[2,32,32,128]{3,2,0,1:T(8,128)(2,1)}), bf16[2,32,32,128]{3,2,0,1:T(8,128)(2,1)S(1)}, u32[]{:S(2)}, u32[]{:S(2)}) %all-to-all-start.1) | async-done | bytes 524320 | tf_op jit(solution)/shard_map/all_to_all | solution.py:298
  38.3 70.4 %shard_map.110 = (bf16[80,64,256]{2,1,0:T(8,128)(2,1)S(1)}, f32[2,64,128]{2,1,0:T(8,128)S(1)}) custom-call(bf16[64,32,128]{2,1,0:T(8,128)(2,1)S(1)} %bitcast.57, s32[4,80,256]{2,1,0:T(8,128)S(1)} %copy-done.4, f32[4,80,256]{2,1,0:T(8,128)S(1)} %copy-done.5, f32[64,1]{1,0:T(8,128)S(1)} %copy.42.bias_ref), custom_call_target="tpu_custom_call" | custom-call | tf_op jit(solution)/shard_map/pallas_call | solution.py:157
  108.8 1.4 collective-permute-start.1
  110.2 5.1 %collective-permute-start = (bf16[64,256]{1,0:T(8,128)(2,1)S(1)}, bf16[64,256]{1,0:T(8,128)(2,1)S(1)}, u32[]{:S(2)}, u32[]{:S(2)}) collective-permute-start(bf16[64,256]{1,0:T(8,128)(2,1)S(1)} %get-tuple-element.24), channel_id=1, source_target_pairs={{0,1},{1,2},{2,3},{4,5},{5,6},{6,7},{8,9},{9,10},{10,11},{12,13},{... | collective-permute-start | bytes 98312 | tf_op jit(solution)/shard_map/ppermute | solution.py:242
  115.5 1.4 collective-permute-done.top_ref
  117.2 1.7 collective-permute-start.2
  118.9 2.4 %collective-permute-start.3 = (bf16[64,128]{1,0:T(8,128)(2,1)S(1)}, bf16[64,128]{1,0:T(8,128)(2,1)S(1)}, u32[]{:S(2)}, u32[]{:S(2)}) collective-permute-start(bf16[64,128]{1,0:T(8,128)(2,1)S(1)} %get-tuple-element.27), channel_id=1, source_target_pairs={{0,4},{1,5},{2,6},{3,7},{4,8},{5,9},{6,10},{7,11},{8,12},{9,13},{1... | collective-permute-start | bytes 49160 | tf_op jit(solution)/shard_map/ppermute | solution.py:262
  121.3 0.6 fusion.8
  123.6 1.3 collective-permute-start.5
  124.9 0.6 collective-permute-start.4
  125.6 4.3 %collective-permute-done.4 = bf16[64,128]{1,0:T(8,128)(2,1)S(1)} collective-permute-done((bf16[64,128]{1,0:T(8,128)(2,1)S(1)}, bf16[64,128]{1,0:T(8,128)(2,1)S(1)}, u32[]{:S(2)}, u32[]{:S(2)}) %collective-permute-start.4) | collective-permute-done | bytes 16416 | tf_op jit(solution)/shard_map/ppermute | solution.py:263
  130.0 18.8 %shard_map.111 = (bf16[80,64,256]{2,1,0:T(8,128)(2,1)S(1)}, f32[2,64,128]{2,1,0:T(8,128)S(1)}) custom-call(bf16[80,64,256]{2,1,0:T(8,128)(2,1)S(1)} %get-tuple-element.9.x_ref.rest_0_, bf16[64,256]{1,0:T(8,128)(2,1)S(1)} %collective-permute-done.top_ref, bf16[64,256]{1,0:T(8,128)(2,1)S(1)} %collective-permute-done.1.bottom_ref, ...), custom_call_target="tpu_custom_call" | custom-call | tf_op jit(solution)/shard_map/pallas_call | solution.py:226
  148.9 1.5 copy-done.1
  150.4 1.3 collective-permute-start.7
  151.7 4.5 %collective-permute-start.6 = (bf16[64,256]{1,0:T(8,128)(2,1)S(1)}, bf16[64,256]{1,0:T(8,128)(2,1)S(1)}, u32[]{:S(2)}, u32[]{:S(2)}) collective-permute-start(bf16[64,256]{1,0:T(8,128)(2,1)S(1)} %get-tuple-element.22), channel_id=1, source_target_pairs={{0,1},{1,2},{2,3},{4,5},{5,6},{6,7},{8,9},{9,10},{10,11},{12,13},{... | collective-permute-start | bytes 98312 | tf_op jit(solution)/shard_map/ppermute | solution.py:242
  156.4 1.4 collective-permute-done.6.top_ref
  158.1 0.6 collective-permute-start.9
  159.1 2.8 %collective-permute-start.11 = (bf16[64,128]{1,0:T(8,128)(2,1)S(1)}, bf16[64,128]{1,0:T(8,128)(2,1)S(1)}, u32[]{:S(2)}, u32[]{:S(2)}) collective-permute-start(bf16[64,128]{1,0:T(8,128)(2,1)S(1)} %get-tuple-element.26), channel_id=1, source_target_pairs={{0,28},{1,29},{2,30},{3,31},{4,0},{5,1},{6,2},{7,3},{8,4},{9,5},{1... | collective-permute-start | bytes 49160 | tf_op jit(solution)/shard_map/ppermute | solution.py:262
  161.9 2.5 %collective-permute-start.10 = (bf16[64,128]{1,0:T(8,128)(2,1)S(1)}, bf16[64,128]{1,0:T(8,128)(2,1)S(1)}, u32[]{:S(2)}, u32[]{:S(2)}) collective-permute-start(bf16[64,128]{1,0:T(8,128)(2,1)S(1)} %get-tuple-element.26), channel_id=1, source_target_pairs={{0,31},{1,30},{2,29},{3,28},{4,3},{5,2},{6,1},{7,0},{8,7},{9,6},{1... | collective-permute-start | bytes 49160 | tf_op jit(solution)/shard_map/ppermute | solution.py:263
  164.4 0.6 collective-permute-done.8
  165.1 1.8 collective-permute-done.10
  167.0 1.7 copy-done.2
  168.7 17.9 %shard_map.112 = bf16[80,64,256]{2,1,0:T(8,128)(2,1)S(1)} custom-call(bf16[80,64,256]{2,1,0:T(8,128)(2,1)S(1)} %copy-done.2, bf16[64,256]{1,0:T(8,128)(2,1)S(1)} %collective-permute-done.6.top_ref, bf16[64,256]{1,0:T(8,128)(2,1)S(1)} %collective-permute-done.7.bottom_ref, f32[2,64,128]{2,1,0:T(8,128)S(1)} %maximum_convert_fusion.1.side_ref, ...), custom_call_target="tpu_custom_call" | custom-call | tf_op jit(solution)/shard_map/pallas_call | solution.py:226
  186.6 3.0 %copy.47 = bf16[64,80,256]{2,1,0:T(8,128)(2,1)} copy(bf16[64,80,256]{2,0,1:T(8,128)(2,1)S(1)} %bitcast.56) | data formatting | bytes 5242880 | tf_op jit(solution)/shard_map/transpose | solution.py:311
  (60 shorter events, 2.6 us)
Async XLA Ops:
  0.0 23.8 %copy-start.9 = (f32[64]{0:T(128)S(1)}, f32[64]{0:T(128)}, u32[]{:S(2)}) copy-start(f32[64]{0:T(128)} %param.17) | copy-start | bytes 772
  1.4 14.4 %all-to-all-start = ((s32[2,1,32]{0,1,2:T(1,128)}), s32[2,1,32]{0,1,2:T(1,128)S(1)}, u32[]{:S(2)}, u32[]{:S(2)}) async-start(s32[2,1,32]{0,1,2:T(1,128)} %copy.37), calls=%async_computation | async-start | bytes 32768 | tf_op jit(solution)/shard_map/all_to_all | solution.py:294
  15.9 1.2 copy-start.3
  17.2 21.1 %copy-start.4 = (s32[4,80,256]{2,1,0:T(8,128)S(1)}, s32[4,80,256]{2,1,0:T(8,128)}, u32[]{:S(2)}) copy-start(s32[4,80,256]{2,1,0:T(8,128)} %cells_ref.1) | copy-start | bytes 983044
  17.2 21.1 %copy-start.5 = (f32[4,80,256]{2,1,0:T(8,128)S(1)}, f32[4,80,256]{2,1,0:T(8,128)}, u32[]{:S(2)}) copy-start(f32[4,80,256]{2,1,0:T(8,128)} %weights_ref.1) | copy-start | bytes 983044
  20.3 100.9 %copy-start.8 = (s32[8]{0:T(128)S(1)}, s32[8]{0:T(128)}, u32[]{:S(2)}) copy-start(s32[8]{0:T(128)} %param.15) | copy-start | bytes 100
  20.4 102.9 %copy-start.10 = (f32[64]{0:T(128)S(1)}, f32[64]{0:T(128)}, u32[]{:S(2)}) copy-start(f32[64]{0:T(128)} %param.19) | copy-start | bytes 772
  20.4 103.0 %copy-start.6 = (bf16[3,3,64,64]{3,2,1,0:T(8,128)(2,1)S(1)}, bf16[3,3,64,64]{3,2,1,0:T(8,128)(2,1)}, u32[]{:S(2)}) copy-start(bf16[3,3,64,64]{3,2,1,0:T(8,128)(2,1)} %param.18) | copy-start | bytes 221188
  21.2 17.0 %all-to-all-start.1 = ((bf16[2,32,32,128]{3,2,0,1:T(8,128)(2,1)}), bf16[2,32,32,128]{3,2,0,1:T(8,128)(2,1)S(1)}, u32[]{:S(2)}, u32[]{:S(2)}) async-start(bf16[2,32,32,128]{3,2,0,1:T(8,128)(2,1)} %copy.40), calls=%async_computation.1 | async-start | bytes 1048576 | tf_op jit(solution)/shard_map/all_to_all | solution.py:298
  108.7 50.4 %copy-start = (bf16[80,64,256]{2,1,0:T(8,128)(2,1)}, bf16[80,64,256]{2,1,0:T(8,128)(2,1)S(1)}, u32[]{:S(2)}) copy-start(bf16[80,64,256]{2,1,0:T(8,128)(2,1)S(1)} %get-tuple-element.9.x_ref.rest_0_) | copy-start | bytes 7864324
  108.7 50.0 %copy-start.11 = (f32[64]{0:T(128)S(1)}, f32[64]{0:T(128)}, u32[]{:S(2)}) copy-start(f32[64]{0:T(128)} %param.21) | copy-start | bytes 772
  108.7 50.1 %copy-start.7 = (bf16[3,3,64,64]{3,2,1,0:T(8,128)(2,1)S(1)}, bf16[3,3,64,64]{3,2,1,0:T(8,128)(2,1)}, u32[]{:S(2)}) copy-start(bf16[3,3,64,64]{3,2,1,0:T(8,128)(2,1)} %param.20) | copy-start | bytes 221188
  108.8 6.6 %collective-permute-start.1 = (bf16[64,256]{1,0:T(8,128)(2,1)S(1)}, bf16[64,256]{1,0:T(8,128)(2,1)S(1)}, u32[]{:S(2)}, u32[]{:S(2)}) collective-permute-start(bf16[64,256]{1,0:T(8,128)(2,1)S(1)} %get-tuple-element.23), channel_id=1, source_target_pairs={{1,0},{2,1},{3,2},{5,4},{6,5},{7,6},{9,8},{10,9},{11,10},{13,12},{... | collective-permute-start | bytes 98312 | tf_op jit(solution)/shard_map/ppermute | solution.py:243
  110.2 6.7 %collective-permute-start = (bf16[64,256]{1,0:T(8,128)(2,1)S(1)}, bf16[64,256]{1,0:T(8,128)(2,1)S(1)}, u32[]{:S(2)}, u32[]{:S(2)}) collective-permute-start(bf16[64,256]{1,0:T(8,128)(2,1)S(1)} %get-tuple-element.24), channel_id=1, source_target_pairs={{0,1},{1,2},{2,3},{4,5},{5,6},{6,7},{8,9},{9,10},{10,11},{12,13},{... | collective-permute-start | bytes 98312 | tf_op jit(solution)/shard_map/ppermute | solution.py:242
  117.2 8.3 %collective-permute-start.2 = (bf16[64,128]{1,0:T(8,128)(2,1)S(1)}, bf16[64,128]{1,0:T(8,128)(2,1)S(1)}, u32[]{:S(2)}, u32[]{:S(2)}) collective-permute-start(bf16[64,128]{1,0:T(8,128)(2,1)S(1)} %get-tuple-element.27), channel_id=1, source_target_pairs={{0,7},{1,6},{2,5},{3,4},{4,11},{5,10},{6,9},{7,8},{8,15},{9,14},{1... | collective-permute-start | bytes 49160 | tf_op jit(solution)/shard_map/ppermute | solution.py:263
  118.9 6.7 %collective-permute-start.3 = (bf16[64,128]{1,0:T(8,128)(2,1)S(1)}, bf16[64,128]{1,0:T(8,128)(2,1)S(1)}, u32[]{:S(2)}, u32[]{:S(2)}) collective-permute-start(bf16[64,128]{1,0:T(8,128)(2,1)S(1)} %get-tuple-element.27), channel_id=1, source_target_pairs={{0,4},{1,5},{2,6},{3,7},{4,8},{5,9},{6,10},{7,11},{8,12},{9,13},{1... | collective-permute-start | bytes 49160 | tf_op jit(solution)/shard_map/ppermute | solution.py:262
  123.6 6.3 %collective-permute-start.5 = (bf16[64,128]{1,0:T(8,128)(2,1)S(1)}, bf16[64,128]{1,0:T(8,128)(2,1)S(1)}, u32[]{:S(2)}, u32[]{:S(2)}) collective-permute-start(bf16[64,128]{1,0:T(8,128)(2,1)S(1)} %get-tuple-element.28), channel_id=1, source_target_pairs={{0,28},{1,29},{2,30},{3,31},{4,0},{5,1},{6,2},{7,3},{8,4},{9,5},{1... | collective-permute-start | bytes 49160 | tf_op jit(solution)/shard_map/ppermute | solution.py:262
  124.9 5.0 %collective-permute-start.4 = (bf16[64,128]{1,0:T(8,128)(2,1)S(1)}, bf16[64,128]{1,0:T(8,128)(2,1)S(1)}, u32[]{:S(2)}, u32[]{:S(2)}) collective-permute-start(bf16[64,128]{1,0:T(8,128)(2,1)S(1)} %get-tuple-element.28), channel_id=1, source_target_pairs={{0,31},{1,30},{2,29},{3,28},{4,3},{5,2},{6,1},{7,0},{8,7},{9,6},{1... | collective-permute-start | bytes 49160 | tf_op jit(solution)/shard_map/ppermute | solution.py:263
  148.9 1.5 copy-start.1
  150.4 5.9 %collective-permute-start.7 = (bf16[64,256]{1,0:T(8,128)(2,1)S(1)}, bf16[64,256]{1,0:T(8,128)(2,1)S(1)}, u32[]{:S(2)}, u32[]{:S(2)}) collective-permute-start(bf16[64,256]{1,0:T(8,128)(2,1)S(1)} %get-tuple-element.21), channel_id=1, source_target_pairs={{1,0},{2,1},{3,2},{5,4},{6,5},{7,6},{9,8},{10,9},{11,10},{13,12},{... | collective-permute-start | bytes 98312 | tf_op jit(solution)/shard_map/ppermute | solution.py:243
  151.7 6.1 %collective-permute-start.6 = (bf16[64,256]{1,0:T(8,128)(2,1)S(1)}, bf16[64,256]{1,0:T(8,128)(2,1)S(1)}, u32[]{:S(2)}, u32[]{:S(2)}) collective-permute-start(bf16[64,256]{1,0:T(8,128)(2,1)S(1)} %get-tuple-element.22), channel_id=1, source_target_pairs={{0,1},{1,2},{2,3},{4,5},{5,6},{6,7},{8,9},{9,10},{10,11},{12,13},{... | collective-permute-start | bytes 98312 | tf_op jit(solution)/shard_map/ppermute | solution.py:242
  158.1 6.9 %collective-permute-start.8 = (bf16[64,128]{1,0:T(8,128)(2,1)S(1)}, bf16[64,128]{1,0:T(8,128)(2,1)S(1)}, u32[]{:S(2)}, u32[]{:S(2)}) collective-permute-start(bf16[64,128]{1,0:T(8,128)(2,1)S(1)} %get-tuple-element.25), channel_id=1, source_target_pairs={{0,7},{1,6},{2,5},{3,4},{4,11},{5,10},{6,9},{7,8},{8,15},{9,14},{1... | collective-permute-start | bytes 49160 | tf_op jit(solution)/shard_map/ppermute | solution.py:263
  158.1 6.9 %collective-permute-start.9 = (bf16[64,128]{1,0:T(8,128)(2,1)S(1)}, bf16[64,128]{1,0:T(8,128)(2,1)S(1)}, u32[]{:S(2)}, u32[]{:S(2)}) collective-permute-start(bf16[64,128]{1,0:T(8,128)(2,1)S(1)} %get-tuple-element.25), channel_id=1, source_target_pairs={{0,4},{1,5},{2,6},{3,7},{4,8},{5,9},{6,10},{7,11},{8,12},{9,13},{1... | collective-permute-start | bytes 49160 | tf_op jit(solution)/shard_map/ppermute | solution.py:262
  159.1 7.8 %collective-permute-start.11 = (bf16[64,128]{1,0:T(8,128)(2,1)S(1)}, bf16[64,128]{1,0:T(8,128)(2,1)S(1)}, u32[]{:S(2)}, u32[]{:S(2)}) collective-permute-start(bf16[64,128]{1,0:T(8,128)(2,1)S(1)} %get-tuple-element.26), channel_id=1, source_target_pairs={{0,28},{1,29},{2,30},{3,31},{4,0},{5,1},{6,2},{7,3},{8,4},{9,5},{1... | collective-permute-start | bytes 49160 | tf_op jit(solution)/shard_map/ppermute | solution.py:262
  161.9 5.0 %collective-permute-start.10 = (bf16[64,128]{1,0:T(8,128)(2,1)S(1)}, bf16[64,128]{1,0:T(8,128)(2,1)S(1)}, u32[]{:S(2)}, u32[]{:S(2)}) collective-permute-start(bf16[64,128]{1,0:T(8,128)(2,1)S(1)} %get-tuple-element.26), channel_id=1, source_target_pairs={{0,31},{1,30},{2,29},{3,28},{4,3},{5,2},{6,1},{7,0},{8,7},{9,6},{1... | collective-permute-start | bytes 49160 | tf_op jit(solution)/shard_map/ppermute | solution.py:263
  167.0 1.7 copy-start.2

commit v3 on v2

--- a/solution.py
+++ b/solution.py
@@ -169,18 +169,23 @@
 
 def conv_kernel(last, x_ref, top_ref, bottom_ref, side_ref, matrix_ref, bias_ref, *rest):
     if last:
-        residual_ref, out_ref, taps = rest
+        residual_ref, out_ref, stack = rest
     else:
-        out_ref, edge_ref, taps = rest
+        out_ref, edge_ref, stack = rest
         edge_ref[...] = jnp.zeros_like(edge_ref)
     rows, channels, cols = x_ref.shape
     lane = lax.broadcasted_iota(jnp.int32, (channels, cols), 1)
     side_lane = lax.broadcasted_iota(jnp.int32, (channels, LANES), 1)
 
-    def multiply(p, row):
+    def place(p, row):
         wide = row.astype(jnp.float32)
+        at = jnp.full((channels, LANES), p, jnp.int32)
         picked = [
-            jnp.sum(jnp.where(side_lane == p, side_ref[s], 0.0), axis=1, keepdims=True)
+            jnp.concatenate(
+                [jnp.take_along_axis(side_ref[s], at, axis=1, mode="promise_in_bounds")]
+                * (cols // LANES),
+                axis=1,
+            )
             for s in range(2)
         ]
         left = jnp.where(lane == 0, picked[0], pltpu.roll(wide, 1, 1))
@@ -188,22 +193,21 @@
         beside = jnp.concatenate(
             (left.astype(jnp.bfloat16), row, right.astype(jnp.bfloat16)), axis=0
         )
-        taps[p] = jnp.dot(matrix_ref[...], beside, preferred_element_type=jnp.float32)
-
-    multiply(0, top_ref[...])
-    multiply(rows + 1, bottom_ref[...])
+        stack[p] = beside
+
+    place(0, top_ref[...])
+    place(rows + 1, bottom_ref[...])
 
     def fill(r, carry):
-        multiply(r + 1, x_ref[r])
-        return carry
-
-    lax.fori_loop(0, rows, fill, 0, unroll=4)
+        place(r + 1, x_ref[r])
+        return carry
+
+    lax.fori_loop(0, rows, fill, 0, unroll=16)
 
     def one_row(r, carry):
-        summed = bias_ref[...] + (
-            taps[r, :channels]
-            + taps[r + 1, channels : 2 * channels]
-            + taps[r + 2, 2 * channels :]
+        window = stack[pl.ds(r, 3)].reshape(9 * channels, cols)
+        summed = bias_ref[...] + jnp.dot(
+            matrix_ref[...], window, preferred_element_type=jnp.float32
         )
         if last:
             out_ref[r] = (summed + residual_ref[r].astype(jnp.float32)).astype(jnp.bfloat16)
@@ -214,7 +218,7 @@
             edge_insert(edge_ref, 1, r, hidden[:, cols - 1 :])
         return carry
 
-    lax.fori_loop(0, rows, one_row, 0, unroll=4)
+    lax.fori_loop(0, rows, one_row, 0, unroll=16)
 
 
 def conv(x, halo, matrix, bias, residual=None):
@@ -228,7 +232,7 @@
         out_shape=grid_shape if last else (grid_shape, edge_shape),
         in_specs=[vmem()] * len(operands),
         out_specs=vmem() if last else (vmem(), vmem()),
-        scratch_shapes=[pltpu.VMEM((rows + 2, 3 * channels, cols), jnp.float32)],
+        scratch_shapes=[pltpu.VMEM((rows + 2, 3 * channels, cols), jnp.bfloat16)],
         compiler_params=params(),
     )(*operands)
 
@@ -274,8 +278,7 @@
 
 
 def kernel_matrix(kernel):
-    size = kernel.shape[0] * kernel.shape[2]
-    return jnp.transpose(kernel, (0, 2, 1, 3)).reshape(size, -1)
+    return jnp.transpose(kernel, (2, 0, 1, 3)).reshape(kernel.shape[2], -1)
 
 
 def shards(

time: 190 us -> 172 us (0.905)
  Pallas kernels: 110 us -> 91.9 us
    pallas_call x2, Pallas kernels: 36.7 us -> 18.4 us  [conv(): pl.pallas_call(functools.partial(conv_kernel, last), out_shape=grid_shape...]
where the time goes in v3:
time: 172 us; the launch traced here: 171 us
  Pallas kernels  91.9 us (53%)
  starting transfers between devices  34.2 us (20%)
  waiting for transfers between devices  29.9 us (17%)
  local copies, waits for them, and re-layouts  13.3 us (8%)
    pallas_call x1, Pallas kernels, lookup(): pl.pallas_call(lookup_kernel, out_shape=(jax.ShapeDtypeStruct((rows, chan...  70.4 us
    pallas_call x2, Pallas kernels, conv(): pl.pallas_call(functools.partial(conv_kernel, last), out_shape=grid_shape...  18.4 us
    all_to_all x1, waiting for transfers between devices, shards(): lax.all_to_all(chosen, ('tile', 'sub'), split_axis=1, concat_axis=1, tile...  14.3 us
    ppermute x2, starting transfers between devices, halos(): top = lax.ppermute(x[rows - 1], 'sub', down)  9.65 us
    all_to_all x1, starting transfers between devices, shards(): lax.all_to_all(fetch_blocks, ('tile', 'sub'), split_axis=2, concat_axis=1...  7.3 us
    ppermute x4, starting transfers between devices, side(): lax.ppermute(edge, ('tile', 'sub'), straight)  7.03 us
    unnamed x26, local copies, waits for them, and re-layouts  6.7 us
    ppermute x4, waiting for transfers between devices, side(): lax.ppermute(edge, ('tile', 'sub'), mirrored)  6.6 us
  transfers between devices with their start and end apart: 14, of which 7 were waited for; matrix products, arithmetic and copies ran while one was open for 2% of the time, Pallas kernels for 0%

profile of v3, /device:TPU:0, one launch (start us, length us, event | category | flops | bytes accessed | tf_op | source)
XLA Modules:
  0.0 171.2 jit_solution(13404499013722530052)
XLA Ops:
  0.0 1.4 copy.41
  1.4 7.3 %all-to-all-start = ((s32[2,1,32]{0,1,2:T(1,128)}), s32[2,1,32]{0,1,2:T(1,128)S(1)}, u32[]{:S(2)}, u32[]{:S(2)}) async-start(s32[2,1,32]{0,1,2:T(1,128)} %copy.41), calls=%async_computation | async-start | bytes 32768 | tf_op jit(solution)/shard_map/all_to_all | solution.py:297
  8.7 0.8 copy.43.weight_ref
  9.5 6.3 %all-to-all-done = s32[2,1,32]{0,1,2:T(1,128)S(1)} async-done(((s32[2,1,32]{0,1,2:T(1,128)}), s32[2,1,32]{0,1,2:T(1,128)S(1)}, u32[]{:S(2)}, u32[]{:S(2)}) %all-to-all-start) | async-done | bytes 288 | tf_op jit(solution)/shard_map/all_to_all | solution.py:297
  15.9 1.2 copy-done.3
  17.2 3.2 %shard_map.109 = bf16[64,32,128]{2,1,0:T(8,128)(2,1)S(1)} custom-call(s32[64]{0:T(128)S(1)} %reshape.27.wanted_ref, bf16[4096,128]{1,0:T(8,128)(2,1)S(1)} %copy-done.3, bf16[128,64]{1,0:T(8,128)(2,1)S(1)} %copy.43.weight_ref), custom_call_target="tpu_custom_call" | custom-call | tf_op jit(solution)/shard_map/pallas_call | solution.py:59
  20.4 0.9 copy.44
  21.2 2.6 %all-to-all-start.1 = ((bf16[2,32,32,128]{3,2,0,1:T(8,128)(2,1)}), bf16[2,32,32,128]{3,2,0,1:T(8,128)(2,1)S(1)}, u32[]{:S(2)}, u32[]{:S(2)}) async-start(bf16[2,32,32,128]{3,2,0,1:T(8,128)(2,1)} %copy.44), calls=%async_computation.1 | async-start | bytes 1048576 | tf_op jit(solution)/shard_map/all_to_all | solution.py:301
  24.0 14.3 %all-to-all-done.1 = bf16[2,32,32,128]{3,2,0,1:T(8,128)(2,1)S(1)} async-done(((bf16[2,32,32,128]{3,2,0,1:T(8,128)(2,1)}), bf16[2,32,32,128]{3,2,0,1:T(8,128)(2,1)S(1)}, u32[]{:S(2)}, u32[]{:S(2)}) %all-to-all-start.1) | async-done | bytes 524320 | tf_op jit(solution)/shard_map/all_to_all | solution.py:301
  38.3 70.4 %shard_map.110 = (bf16[80,64,256]{2,1,0:T(8,128)(2,1)S(1)}, f32[2,64,128]{2,1,0:T(8,128)S(1)}) custom-call(bf16[64,32,128]{2,1,0:T(8,128)(2,1)S(1)} %bitcast.59, s32[4,80,256]{2,1,0:T(8,128)S(1)} %copy-done.4, f32[4,80,256]{2,1,0:T(8,128)S(1)} %copy-done.5, f32[64,1]{1,0:T(8,128)S(1)} %copy.46.bias_ref), custom_call_target="tpu_custom_call" | custom-call | tf_op jit(solution)/shard_map/pallas_call | solution.py:157
  108.8 1.4 collective-permute-start.1
  110.2 5.1 %collective-permute-start = (bf16[64,256]{1,0:T(8,128)(2,1)S(1)}, bf16[64,256]{1,0:T(8,128)(2,1)S(1)}, u32[]{:S(2)}, u32[]{:S(2)}) collective-permute-start(bf16[64,256]{1,0:T(8,128)(2,1)S(1)} %get-tuple-element.24), channel_id=1, source_target_pairs={{0,1},{1,2},{2,3},{4,5},{5,6},{6,7},{8,9},{9,10},{10,11},{12,13},{... | collective-permute-start | bytes 98312 | tf_op jit(solution)/shard_map/ppermute | solution.py:246
  115.5 1.4 collective-permute-done.top_ref
  117.2 1.7 collective-permute-start.2
  118.9 2.4 %collective-permute-start.3 = (bf16[64,128]{1,0:T(8,128)(2,1)S(1)}, bf16[64,128]{1,0:T(8,128)(2,1)S(1)}, u32[]{:S(2)}, u32[]{:S(2)}) collective-permute-start(bf16[64,128]{1,0:T(8,128)(2,1)S(1)} %get-tuple-element.27), channel_id=1, source_target_pairs={{0,4},{1,5},{2,6},{3,7},{4,8},{5,9},{6,10},{7,11},{8,12},{9,13},{1... | collective-permute-start | bytes 49160 | tf_op jit(solution)/shard_map/ppermute | solution.py:266
  121.3 0.6 fusion.8
  123.6 1.3 collective-permute-start.5
  124.9 0.6 collective-permute-start.4
  125.6 4.3 %collective-permute-done.4 = bf16[64,128]{1,0:T(8,128)(2,1)S(1)} collective-permute-done((bf16[64,128]{1,0:T(8,128)(2,1)S(1)}, bf16[64,128]{1,0:T(8,128)(2,1)S(1)}, u32[]{:S(2)}, u32[]{:S(2)}) %collective-permute-start.4) | collective-permute-done | bytes 16416 | tf_op jit(solution)/shard_map/ppermute | solution.py:267
  130.0 8.6 %shard_map.111 = (bf16[80,64,256]{2,1,0:T(8,128)(2,1)S(1)}, f32[2,64,128]{2,1,0:T(8,128)S(1)}) custom-call(bf16[80,64,256]{2,1,0:T(8,128)(2,1)S(1)} %get-tuple-element.9.x_ref.rest_0_, bf16[64,256]{1,0:T(8,128)(2,1)S(1)} %collective-permute-done.top_ref, bf16[64,256]{1,0:T(8,128)(2,1)S(1)} %collective-permute-done.1.bottom_ref, ...), custom_call_target="tpu_custom_call" | custom-call | tf_op jit(solution)/shard_map/pallas_call | solution.py:230
  138.6 1.5 copy-done.1
  140.1 1.3 collective-permute-start.7
  141.4 4.5 %collective-permute-start.6 = (bf16[64,256]{1,0:T(8,128)(2,1)S(1)}, bf16[64,256]{1,0:T(8,128)(2,1)S(1)}, u32[]{:S(2)}, u32[]{:S(2)}) collective-permute-start(bf16[64,256]{1,0:T(8,128)(2,1)S(1)} %get-tuple-element.22), channel_id=1, source_target_pairs={{0,1},{1,2},{2,3},{4,5},{5,6},{6,7},{8,9},{9,10},{10,11},{12,13},{... | collective-permute-start | bytes 98312 | tf_op jit(solution)/shard_map/ppermute | solution.py:246
  146.1 1.4 collective-permute-done.6.top_ref
  147.9 0.6 collective-permute-start.9
  148.9 2.8 %collective-permute-start.11 = (bf16[64,128]{1,0:T(8,128)(2,1)S(1)}, bf16[64,128]{1,0:T(8,128)(2,1)S(1)}, u32[]{:S(2)}, u32[]{:S(2)}) collective-permute-start(bf16[64,128]{1,0:T(8,128)(2,1)S(1)} %get-tuple-element.26), channel_id=1, source_target_pairs={{0,28},{1,29},{2,30},{3,31},{4,0},{5,1},{6,2},{7,3},{8,4},{9,5},{1... | collective-permute-start | bytes 49160 | tf_op jit(solution)/shard_map/ppermute | solution.py:266
  151.6 2.5 %collective-permute-start.10 = (bf16[64,128]{1,0:T(8,128)(2,1)S(1)}, bf16[64,128]{1,0:T(8,128)(2,1)S(1)}, u32[]{:S(2)}, u32[]{:S(2)}) collective-permute-start(bf16[64,128]{1,0:T(8,128)(2,1)S(1)} %get-tuple-element.26), channel_id=1, source_target_pairs={{0,31},{1,30},{2,29},{3,28},{4,3},{5,2},{6,1},{7,0},{8,7},{9,6},{1... | collective-permute-start | bytes 49160 | tf_op jit(solution)/shard_map/ppermute | solution.py:267
  154.2 0.6 collective-permute-done.8
  154.8 1.8 %collective-permute-done.10 = bf16[64,128]{1,0:T(8,128)(2,1)S(1)} collective-permute-done((bf16[64,128]{1,0:T(8,128)(2,1)S(1)}, bf16[64,128]{1,0:T(8,128)(2,1)S(1)}, u32[]{:S(2)}, u32[]{:S(2)}) %collective-permute-start.10) | collective-permute-done | bytes 16416 | tf_op jit(solution)/shard_map/ppermute | solution.py:267
  156.7 1.7 %copy-done.2 = bf16[80,64,256]{2,1,0:T(8,128)(2,1)S(1)} copy-done((bf16[80,64,256]{2,1,0:T(8,128)(2,1)S(1)}, bf16[80,64,256]{2,1,0:T(8,128)(2,1)}, u32[]{:S(2)}) %copy-start.2) | copy-done | bytes 2621464
  158.5 9.8 %shard_map.112 = bf16[80,64,256]{2,1,0:T(8,128)(2,1)S(1)} custom-call(bf16[80,64,256]{2,1,0:T(8,128)(2,1)S(1)} %copy-done.2, bf16[64,256]{1,0:T(8,128)(2,1)S(1)} %collective-permute-done.6.top_ref, bf16[64,256]{1,0:T(8,128)(2,1)S(1)} %collective-permute-done.7.bottom_ref, f32[2,64,128]{2,1,0:T(8,128)S(1)} %maximum_convert_fusion.1.side_ref, ...), custom_call_target="tpu_custom_call" | custom-call | tf_op jit(solution)/shard_map/pallas_call | solution.py:230
  168.3 3.0 %copy.53 = bf16[64,80,256]{2,1,0:T(8,128)(2,1)} copy(bf16[64,80,256]{2,0,1:T(8,128)(2,1)S(1)} %bitcast.58) | data formatting | bytes 5242880 | tf_op jit(solution)/shard_map/transpose | solution.py:314
  (60 shorter events, 2.6 us)
Async XLA Ops:
  0.0 23.8 %copy-start.9 = (f32[64]{0:T(128)S(1)}, f32[64]{0:T(128)}, u32[]{:S(2)}) copy-start(f32[64]{0:T(128)} %param.17) | copy-start | bytes 772
  1.4 14.4 %all-to-all-start = ((s32[2,1,32]{0,1,2:T(1,128)}), s32[2,1,32]{0,1,2:T(1,128)S(1)}, u32[]{:S(2)}, u32[]{:S(2)}) async-start(s32[2,1,32]{0,1,2:T(1,128)} %copy.41), calls=%async_computation | async-start | bytes 32768 | tf_op jit(solution)/shard_map/all_to_all | solution.py:297
  15.9 1.2 copy-start.3
  17.2 21.1 %copy-start.4 = (s32[4,80,256]{2,1,0:T(8,128)S(1)}, s32[4,80,256]{2,1,0:T(8,128)}, u32[]{:S(2)}) copy-start(s32[4,80,256]{2,1,0:T(8,128)} %cells_ref.1) | copy-start | bytes 983044
  17.2 21.1 %copy-start.5 = (f32[4,80,256]{2,1,0:T(8,128)S(1)}, f32[4,80,256]{2,1,0:T(8,128)}, u32[]{:S(2)}) copy-start(f32[4,80,256]{2,1,0:T(8,128)} %weights_ref.1) | copy-start | bytes 983044
  20.3 100.9 %copy-start.8 = (s32[8]{0:T(128)S(1)}, s32[8]{0:T(128)}, u32[]{:S(2)}) copy-start(s32[8]{0:T(128)} %param.15) | copy-start | bytes 100
  20.4 102.9 %copy-start.10 = (f32[64]{0:T(128)S(1)}, f32[64]{0:T(128)}, u32[]{:S(2)}) copy-start(f32[64]{0:T(128)} %param.19) | copy-start | bytes 772
  20.4 103.0 %copy-start.6 = (bf16[3,3,64,64]{3,2,1,0:T(8,128)(2,1)S(1)}, bf16[3,3,64,64]{3,2,1,0:T(8,128)(2,1)}, u32[]{:S(2)}) copy-start(bf16[3,3,64,64]{3,2,1,0:T(8,128)(2,1)} %param.18) | copy-start | bytes 221188
  21.2 17.0 %all-to-all-start.1 = ((bf16[2,32,32,128]{3,2,0,1:T(8,128)(2,1)}), bf16[2,32,32,128]{3,2,0,1:T(8,128)(2,1)S(1)}, u32[]{:S(2)}, u32[]{:S(2)}) async-start(bf16[2,32,32,128]{3,2,0,1:T(8,128)(2,1)} %copy.44), calls=%async_computation.1 | async-start | bytes 1048576 | tf_op jit(solution)/shard_map/all_to_all | solution.py:301
  38.3 110.2 %copy-start.11 = (f32[64]{0:T(128)S(1)}, f32[64]{0:T(128)}, u32[]{:S(2)}) copy-start(f32[64]{0:T(128)} %param.21) | copy-start | bytes 772
  108.7 48.0 %copy-start = (bf16[80,64,256]{2,1,0:T(8,128)(2,1)}, bf16[80,64,256]{2,1,0:T(8,128)(2,1)S(1)}, u32[]{:S(2)}) copy-start(bf16[80,64,256]{2,1,0:T(8,128)(2,1)S(1)} %get-tuple-element.9.x_ref.rest_0_) | copy-start | bytes 7864324
  108.7 39.8 %copy-start.7 = (bf16[3,3,64,64]{3,2,1,0:T(8,128)(2,1)S(1)}, bf16[3,3,64,64]{3,2,1,0:T(8,128)(2,1)}, u32[]{:S(2)}) copy-start(bf16[3,3,64,64]{3,2,1,0:T(8,128)(2,1)} %param.20) | copy-start | bytes 221188
  108.8 6.6 %collective-permute-start.1 = (bf16[64,256]{1,0:T(8,128)(2,1)S(1)}, bf16[64,256]{1,0:T(8,128)(2,1)S(1)}, u32[]{:S(2)}, u32[]{:S(2)}) collective-permute-start(bf16[64,256]{1,0:T(8,128)(2,1)S(1)} %get-tuple-element.23), channel_id=1, source_target_pairs={{1,0},{2,1},{3,2},{5,4},{6,5},{7,6},{9,8},{10,9},{11,10},{13,12},{... | collective-permute-start | bytes 98312 | tf_op jit(solution)/shard_map/ppermute | solution.py:247
  110.2 6.7 %collective-permute-start = (bf16[64,256]{1,0:T(8,128)(2,1)S(1)}, bf16[64,256]{1,0:T(8,128)(2,1)S(1)}, u32[]{:S(2)}, u32[]{:S(2)}) collective-permute-start(bf16[64,256]{1,0:T(8,128)(2,1)S(1)} %get-tuple-element.24), channel_id=1, source_target_pairs={{0,1},{1,2},{2,3},{4,5},{5,6},{6,7},{8,9},{9,10},{10,11},{12,13},{... | collective-permute-start | bytes 98312 | tf_op jit(solution)/shard_map/ppermute | solution.py:246
  117.2 8.3 %collective-permute-start.2 = (bf16[64,128]{1,0:T(8,128)(2,1)S(1)}, bf16[64,128]{1,0:T(8,128)(2,1)S(1)}, u32[]{:S(2)}, u32[]{:S(2)}) collective-permute-start(bf16[64,128]{1,0:T(8,128)(2,1)S(1)} %get-tuple-element.27), channel_id=1, source_target_pairs={{0,7},{1,6},{2,5},{3,4},{4,11},{5,10},{6,9},{7,8},{8,15},{9,14},{1... | collective-permute-start | bytes 49160 | tf_op jit(solution)/shard_map/ppermute | solution.py:267
  118.9 6.7 %collective-permute-start.3 = (bf16[64,128]{1,0:T(8,128)(2,1)S(1)}, bf16[64,128]{1,0:T(8,128)(2,1)S(1)}, u32[]{:S(2)}, u32[]{:S(2)}) collective-permute-start(bf16[64,128]{1,0:T(8,128)(2,1)S(1)} %get-tuple-element.27), channel_id=1, source_target_pairs={{0,4},{1,5},{2,6},{3,7},{4,8},{5,9},{6,10},{7,11},{8,12},{9,13},{1... | collective-permute-start | bytes 49160 | tf_op jit(solution)/shard_map/ppermute | solution.py:266
  123.6 6.3 %collective-permute-start.5 = (bf16[64,128]{1,0:T(8,128)(2,1)S(1)}, bf16[64,128]{1,0:T(8,128)(2,1)S(1)}, u32[]{:S(2)}, u32[]{:S(2)}) collective-permute-start(bf16[64,128]{1,0:T(8,128)(2,1)S(1)} %get-tuple-element.28), channel_id=1, source_target_pairs={{0,28},{1,29},{2,30},{3,31},{4,0},{5,1},{6,2},{7,3},{8,4},{9,5},{1... | collective-permute-start | bytes 49160 | tf_op jit(solution)/shard_map/ppermute | solution.py:266
  124.9 5.0 %collective-permute-start.4 = (bf16[64,128]{1,0:T(8,128)(2,1)S(1)}, bf16[64,128]{1,0:T(8,128)(2,1)S(1)}, u32[]{:S(2)}, u32[]{:S(2)}) collective-permute-start(bf16[64,128]{1,0:T(8,128)(2,1)S(1)} %get-tuple-element.28), channel_id=1, source_target_pairs={{0,31},{1,30},{2,29},{3,28},{4,3},{5,2},{6,1},{7,0},{8,7},{9,6},{1... | collective-permute-start | bytes 49160 | tf_op jit(solution)/shard_map/ppermute | solution.py:267
  138.6 1.5 copy-start.1
  140.1 5.9 %collective-permute-start.7 = (bf16[64,256]{1,0:T(8,128)(2,1)S(1)}, bf16[64,256]{1,0:T(8,128)(2,1)S(1)}, u32[]{:S(2)}, u32[]{:S(2)}) collective-permute-start(bf16[64,256]{1,0:T(8,128)(2,1)S(1)} %get-tuple-element.21), channel_id=1, source_target_pairs={{1,0},{2,1},{3,2},{5,4},{6,5},{7,6},{9,8},{10,9},{11,10},{13,12},{... | collective-permute-start | bytes 98312 | tf_op jit(solution)/shard_map/ppermute | solution.py:247
  141.4 6.1 %collective-permute-start.6 = (bf16[64,256]{1,0:T(8,128)(2,1)S(1)}, bf16[64,256]{1,0:T(8,128)(2,1)S(1)}, u32[]{:S(2)}, u32[]{:S(2)}) collective-permute-start(bf16[64,256]{1,0:T(8,128)(2,1)S(1)} %get-tuple-element.22), channel_id=1, source_target_pairs={{0,1},{1,2},{2,3},{4,5},{5,6},{6,7},{8,9},{9,10},{10,11},{12,13},{... | collective-permute-start | bytes 98312 | tf_op jit(solution)/shard_map/ppermute | solution.py:246
  147.8 6.9 %collective-permute-start.8 = (bf16[64,128]{1,0:T(8,128)(2,1)S(1)}, bf16[64,128]{1,0:T(8,128)(2,1)S(1)}, u32[]{:S(2)}, u32[]{:S(2)}) collective-permute-start(bf16[64,128]{1,0:T(8,128)(2,1)S(1)} %get-tuple-element.25), channel_id=1, source_target_pairs={{0,7},{1,6},{2,5},{3,4},{4,11},{5,10},{6,9},{7,8},{8,15},{9,14},{1... | collective-permute-start | bytes 49160 | tf_op jit(solution)/shard_map/ppermute | solution.py:267
  147.9 6.9 %collective-permute-start.9 = (bf16[64,128]{1,0:T(8,128)(2,1)S(1)}, bf16[64,128]{1,0:T(8,128)(2,1)S(1)}, u32[]{:S(2)}, u32[]{:S(2)}) collective-permute-start(bf16[64,128]{1,0:T(8,128)(2,1)S(1)} %get-tuple-element.25), channel_id=1, source_target_pairs={{0,4},{1,5},{2,6},{3,7},{4,8},{5,9},{6,10},{7,11},{8,12},{9,13},{1... | collective-permute-start | bytes 49160 | tf_op jit(solution)/shard_map/ppermute | solution.py:266
  148.9 7.8 %collective-permute-start.11 = (bf16[64,128]{1,0:T(8,128)(2,1)S(1)}, bf16[64,128]{1,0:T(8,128)(2,1)S(1)}, u32[]{:S(2)}, u32[]{:S(2)}) collective-permute-start(bf16[64,128]{1,0:T(8,128)(2,1)S(1)} %get-tuple-element.26), channel_id=1, source_target_pairs={{0,28},{1,29},{2,30},{3,31},{4,0},{5,1},{6,2},{7,3},{8,4},{9,5},{1... | collective-permute-start | bytes 49160 | tf_op jit(solution)/shard_map/ppermute | solution.py:266
  151.6 5.0 %collective-permute-start.10 = (bf16[64,128]{1,0:T(8,128)(2,1)S(1)}, bf16[64,128]{1,0:T(8,128)(2,1)S(1)}, u32[]{:S(2)}, u32[]{:S(2)}) collective-permute-start(bf16[64,128]{1,0:T(8,128)(2,1)S(1)} %get-tuple-element.26), channel_id=1, source_target_pairs={{0,31},{1,30},{2,29},{3,28},{4,3},{5,2},{6,1},{7,0},{8,7},{9,6},{1... | collective-permute-start | bytes 49160 | tf_op jit(solution)/shard_map/ppermute | solution.py:267
  156.7 1.7 %copy-start.2 = (bf16[80,64,256]{2,1,0:T(8,128)(2,1)S(1)}, bf16[80,64,256]{2,1,0:T(8,128)(2,1)}, u32[]{:S(2)}) copy-start(bf16[80,64,256]{2,1,0:T(8,128)(2,1)} %copy-done.1) | copy-start | bytes 7864324
